TPU v7x, 32 devices: a whole 2x2x4 slice. The times are simulated.
32 devices in a mesh: chol: 2 (over x), walk: 16 (over z, y, core).
Axes of the slice: x: 2, y: 2, z: 4, core: 2. Of those that a mesh axis runs over, the one named last changes fastest.
Arguments:
- field_draws: bfloat16 [16, 2048], P('walk', 'chol'), may hold values from -6 to 6
- chol_vectors: bfloat16 [2048, 512, 512], P('chol', 'walk'), as said below
- rotated_vectors: bfloat16 [2048, 128, 512], P(('chol', 'walk')), may hold values from -1.5 to 1.5
- walkers: bfloat16 [16, 512, 128], P('walk'), may hold values from -6 to 6
Outputs:
- propagated: float32 [16, 512, 128], P('walk')
- exchange_energy: float32 [16], P('walk')
Inputs may be any that keep to these rules, and one draw needn't show every extreme that they name: Each chol_vectors[g] is a symmetric matrix.
All inputs are finite; a program needn't handle non-finite values.
Results may differ from a plain program's by a relative error of at most 0.0036.
Values may be sent and summed in bfloat16 or wider, within the bound.
No kernel may reach another device: no remote copies, remote signals or barrier semaphores. Data moves between devices by JAX's collectives and lax.ppermute only.
A program may use at most 192 MiB of HBM per device.

v0:
```python
import jax
import jax.numpy as jnp
from jax import lax
from jax.sharding import PartitionSpec as P

OCC = 128
TERMS = 4


def solve_dual(correlation, transposed):
    gram = jnp.dot(correlation, correlation.T, precision=lax.Precision.HIGHEST)
    factor = jnp.linalg.cholesky(gram)
    right = jnp.dot(correlation, transposed, precision=lax.Precision.HIGHEST)
    return jax.scipy.linalg.cho_solve((factor, True), right)


def energy_folder(rotated_vectors):

    def accumulate(totals, columns, offset):
        walker_count = columns.shape[1] // OCC

        def vector_step(vector, summed):
            single = lax.dynamic_index_in_dim(rotated_vectors, vector, 0, keepdims=False)
            products = jnp.dot(single, columns, preferred_element_type=jnp.float32)
            tiled = products.reshape(OCC, walker_count, OCC)
            return summed + jnp.einsum("iwj,jwi->w", tiled, tiled)

        contrib = lax.fori_loop(
            0, rotated_vectors.shape[0], vector_step, jnp.zeros((walker_count,), jnp.float32)
        )
        return contrib

    return accumulate


def per_device(field_draws, chol_vectors, rotated_vectors, walkers):
    local_walkers = walkers.shape[0]
    walk_count = lax.axis_size("walk")
    total_walkers = local_walkers * walk_count
    slab_vectors, slab_rows, orbitals = chol_vectors.shape
    all_draws = lax.all_gather(field_draws, "walk", axis=0, tiled=True)
    partial_rows = jnp.dot(
        all_draws,
        chol_vectors.reshape(slab_vectors, slab_rows * orbitals),
        preferred_element_type=jnp.float32,
    )
    partial_rows = partial_rows.reshape(total_walkers, slab_rows, orbitals)
    summed_rows = lax.psum(partial_rows, "chol").astype(jnp.bfloat16)
    operators = lax.all_to_all(summed_rows, "walk", split_axis=0, concat_axis=1, tiled=True)
    taylor_term = walkers
    propagated = walkers.astype(jnp.float32)
    for degree in range(1, TERMS + 1):
        applied = jnp.einsum(
            "wpq,wqi->wpi", operators, taylor_term, preferred_element_type=jnp.float32
        )
        taylor_term = (applied / degree).astype(jnp.bfloat16)
        propagated = propagated + taylor_term.astype(jnp.float32)
    correlation = jnp.einsum(
        "wpi,wpj->wij", walkers.astype(jnp.float32), propagated, precision=lax.Precision.HIGHEST
    )
    dual_t = jax.vmap(solve_dual)(correlation, jnp.transpose(propagated, (0, 2, 1)))
    dual_cols = (
        jnp.transpose(dual_t, (2, 0, 1)).reshape(orbitals, local_walkers * OCC).astype(jnp.bfloat16)
    )
    accumulate = energy_folder(rotated_vectors)
    empty = jnp.zeros((total_walkers,), jnp.float32)
    totals = accumulate(empty, lax.all_gather(dual_cols, "walk", axis=1, tiled=True), jnp.int32(0))
    summed = lax.psum(totals, ("chol", "walk"))
    mine = lax.dynamic_slice_in_dim(
        summed, lax.axis_index("walk") * local_walkers, local_walkers, 0
    )
    return (propagated, -0.5 * mine)


def solution(mesh):
    return jax.shard_map(
        per_device,
        mesh=mesh,
        in_specs=(
            P("walk", "chol"),
            P("chol", "walk", None),
            P(("chol", "walk"), None, None),
            P("walk", None, None),
        ),
        out_specs=(P("walk", None, None), P("walk")),
        check_vma=False,
    )
```

profile of v0, /device:TPU:0, one launch (start us, length us, event | category | flops | bytes accessed | tf_op | source)
XLA Modules:
  0.0 477.7 jit_solution(1206323439816212944)
XLA Ops:
  7.2 31.0 %copy.31 = bf16[128,8,32,512]{3,1,2,0:T(8,128)(2,1)} copy(bf16[128,8,32,512]{3,2,1,0:T(8,128)(2,1)} %bitcast.93) | data formatting | bytes 67108864
  38.2 44.0 %copy.19 = bf16[16384,1024]{1,0:T(8,128)(2,1)} copy(bf16[16384,1024]{0,1:T(8,128)(2,1)} %bitcast.90) | data formatting | bytes 67108864 | tf_op jit(solution)/shard_map/dot_general | solution.py:42
  82.2 23.2 %all-gather.1 = bf16[16,1,1024]{2,1,0:T(2,128)(2,1)S(1)} all-gather(bf16[1,1,1024]{2,1,0:T(2,128)(2,1)S(1)} %bitcast.99), channel_id=1, replica_groups=mesh['chol'=2,'walk'=16] {'walk'}, dimensions={0}, use_global_device_ids=true | all-gather | bytes 34816 | tf_op jit(solution)/shard_map/all_gather | solution.py:41
  105.5 14.5 %fusion.23 = f32[16,32,512]{2,0,1:T(8,128)S(1)} fusion(bf16[32,512,1024]{2,1,0:T(8,128)(2,1)} %bitcast.89, bf16[16,1,1024]{2,1,0:T(2,128)(2,1)S(1)} %all-gather.1), kind=kOutput, calls=%fused_computation.38 | convolution fusion | flops 536870912 | bytes 34635776 | tf_op jit(solution)/shard_map/dot_general | solution.py:42
  120.0 30.1 %all-reduce.1 = bf16[16,32,512]{2,0,1:T(8,128)(2,1)S(1)} all-reduce(f32[16,32,512]{2,0,1:T(8,128)S(1)} %fusion.23), channel_id=1, replica_groups=mesh['chol'=2,'walk'=16] {'chol'}, use_global_device_ids=true, to_apply=%region_0.0 | all-reduce | flops 262144 | bytes 1572864 | tf_op jit(solution)/shard_map/psum | solution.py:48
  150.5 17.1 %all_to_all.4 = bf16[16,32,512]{2,1,0:T(8,128)(2,1)S(1)} all-to-all(bf16[16,32,512]{2,1,0:T(8,128)(2,1)S(1)} %copy.20), channel_id=1, replica_groups=mesh['chol'=2,'walk'=16] {'walk'}, dimensions={0} | all-to-all | bytes 1048576 | tf_op jit(solution)/shard_map/all_to_all | solution.py:49
  170.0 11.7 %custom-call.11 = f32[1,128,128]{2,1,0:T(8,128)S(1)} custom-call(f32[1,128,128]{2,1,0:T(8,128)S(1)} %fusion.19), custom_call_target="Cholesky" | custom-call | tf_op jit(solution)/shard_map/vmap(jit(cholesky))/cholesky | solution.py:12
  183.0 9.8 %custom-call.12 = f32[1,1,128,128]{2,3,1,0:T(8,128)S(1)} custom-call(f32[1,1,128,128]{3,2,1,0:T(8,128)S(1)} %fusion.18), custom_call_target="InvertDiagBlocksLowerTriangular" | custom-call | tf_op jit(solution)/shard_map/vmap(jit(_cho_solve))/triangular_solve | solution.py:14
  194.3 39.9 %all-gather.4.cloned.1.call-done = bf16[512,1,2048]{0,2,1:T(8,128)(2,1)} async-done(((bf16[512,1,128]{0,2,1:T(8,128)(2,1)}), bf16[512,1,2048]{0,2,1:T(8,128)(2,1)}) %all-gather.4.cloned.1.call-update) | async-done | bytes 2097168 | tf_op jit(solution)/shard_map/all_gather | solution.py:67
  234.3 195.9 %while.14 = (s32[]{:T(128)}, f32[16]{0:T(128)S(1)}, bf16[64,128,512]{2,1,0:T(8,128)(2,1)}, bf16[512,2048]{0,1:T(8,128)(2,1)}, s32[]{:T(128)}, /*index=5*/s32[]{:T(128)}) while((s32[]{:T(128)}, f32[16]{0:T(128)S(1)}, bf16[64,128,512]{2,1,0:T(8,128)(2,1)}, bf16[512,2048]{0,1:T(8,128)(2,1)}, s32[]{:T(128)}, /*index=5*/s32[]{:T(128)}) %tuple.43), condition=%wide.region_4.5_spmd.clone, body=%wide.region_3.4_spmd.clone.sunk | while | flops 268959776 | bytes 7471951 | solution.py:28
  237.3 2.5 fusion.47
  243.5 2.5 fusion.47
  249.6 2.5 fusion.47
  255.7 2.5 fusion.47
  261.8 2.5 fusion.47
  267.9 2.5 fusion.47
  274.1 2.5 fusion.47
  280.2 2.5 fusion.47
  286.3 2.5 fusion.47
  292.4 2.5 fusion.47
  298.6 2.5 fusion.47
  304.7 2.5 fusion.47
  310.8 2.5 fusion.47
  316.9 2.5 fusion.47
  341.4 2.5 fusion.47
  359.8 2.5 fusion.47
  365.9 2.5 fusion.47
  384.3 2.5 fusion.47
  390.4 2.5 fusion.47
  408.8 2.5 fusion.47
  414.9 2.5 fusion.47
  430.2 38.3 %psum.15 = f32[16]{0:T(128)S(1)} all-reduce(f32[16]{0:T(128)S(1)} %get-tuple-element.81), channel_id=1, replica_groups=mesh['chol'=2,'walk'=16] {'chol','walk'}, use_global_device_ids=true, to_apply=%region_5.6 | all-reduce | flops 16 | bytes 128 | tf_op jit(solution)/shard_map/psum | solution.py:68
  (260 shorter events, 148.6 us)
Async XLA Ops:
  7.2 227.1 %all-gather.4.cloned.1.call-start = ((), (), s32[]{:S(2)}) async-start(), calls=%async_computation.1 | async-start | bytes 2228224 | tf_op jit(solution)/shard_map/all_gather | solution.py:67
  38.2 44.0 %copy-start.2 = (bf16[1,1024]{1,0:T(2,128)(2,1)S(1)}, bf16[1,1024]{1,0:T(2,128)(2,1)}, u32[]{:S(2)}) copy-start(bf16[1,1024]{1,0:T(2,128)(2,1)} %param.6) | copy-start | bytes 6148
  105.5 62.1 %copy-start.1 = (bf16[1,512,128]{2,1,0:T(8,128)(2,1)S(1)}, bf16[1,512,128]{2,1,0:T(8,128)(2,1)}, u32[]{:S(2)}) copy-start(bf16[1,512,128]{2,1,0:T(8,128)(2,1)} %param.9) | copy-start | bytes 393220
  168.7 65.6 %copy-start = (f32[1,512,128]{2,1,0:T(8,128)}, f32[1,512,128]{2,1,0:T(8,128)S(1)}, u32[]{:S(2)}) copy-start(f32[1,512,128]{2,1,0:T(8,128)S(1)} %fusion.10) | copy-start | bytes 786436
Sparse Core Ops, SparseCore 0:
  194.4 39.7 all-gather.3
where the time goes:
time: 481 us; the launch traced here: 478 us
  matrix products  177 us (37%)
  blocking collectives  109 us (23%)
  local copies, waits for them, and re-layouts  97.2 us (20%)
  waiting for transfers between devices  40 us (8%)
  other arithmetic  37.7 us (8%)
  between operations  15.9 us (3%)
    dot_general x64, matrix products, vector_step(): products = jnp.dot(single, columns, preferred_element_type=jnp.float32)  158 us
    dot_general x1, local copies, waits for them, and re-layouts, per_device(): jnp.dot(all_draws, chol_vectors.reshape(slab_vectors, slab_rows * orbital...  44 us
    all_gather x1, waiting for transfers between devices, per_device(): lax.all_gather(dual_cols, 'walk', axis=1, tiled=True)  39.9 us
    psum x1, blocking collectives, per_device(): summed = lax.psum(totals, ('chol', 'walk'))  38.3 us
    unnamed x7, local copies, waits for them, and re-layouts  31 us
    psum x1, blocking collectives, per_device(): summed_rows = lax.psum(partial_rows, 'chol').astype(jnp.bfloat16)  30.1 us
    all_gather x1, blocking collectives, per_device(): all_draws = lax.all_gather(field_draws, 'walk', axis=0, tiled=True)  23.2 us
    while x64, local copies, waits for them, and re-layouts  21.2 us
  transfers between devices with their start and end apart: 1, of which 1 were waited for; matrix products, arithmetic and copies ran while one was open for 0% of the time, Pallas kernels for 0%

commit v1 on v0

v1 whole, which is shorter than its diff:
```python
import functools

import jax
import jax.numpy as jnp
from jax import lax
from jax.experimental import pallas as pl
from jax.experimental.pallas import tpu as pltpu
from jax.sharding import PartitionSpec as P

TERMS = 4
TILE = 16
BF = jnp.bfloat16
F32 = jnp.float32
BOTH = ("chol", "walk")


def solve_dual(correlation, transposed):
    gram = jnp.dot(correlation, correlation.T, precision=lax.Precision.HIGHEST)
    factor = jnp.linalg.cholesky(gram)
    right = jnp.dot(correlation, transposed, precision=lax.Precision.HIGHEST)
    return jax.scipy.linalg.cho_solve((factor, True), right)


def propagate(operators, walkers):
    taylor_term = walkers
    propagated = walkers.astype(F32)
    for degree in range(1, TERMS + 1):
        applied = jnp.dot(operators, taylor_term, preferred_element_type=F32)
        taylor_term = (applied / degree).astype(BF)
        propagated = propagated + taylor_term.astype(F32)
    return propagated


def dual_of(walkers, propagated):
    correlation = jnp.dot(walkers.astype(F32).T, propagated, precision=lax.Precision.HIGHEST)
    return solve_dual(correlation, propagated.T).T.astype(BF)


def operator_kernel(planes, draws_ref, chol_ref, out_ref, acc_ref, spread_ref):
    step = pl.program_id(0)
    walkers, group = draws_ref.shape[1:]
    rows, orbitals = chol_ref.shape[1:]
    depth = group * TILE

    @pl.when(step == 0)
    def _():
        acc_ref[...] = jnp.zeros_like(acc_ref)

    owner = lax.broadcasted_iota(jnp.int32, (group, depth), 1) // TILE
    repeat = jnp.where(owner == lax.broadcasted_iota(jnp.int32, (group, depth), 0), 1.0, 0.0).astype(BF)
    repeated = jnp.dot(draws_ref[0], repeat, preferred_element_type=F32)
    lane_row = lax.broadcasted_iota(jnp.int32, (TILE, depth), 1) % TILE
    diagonal = lane_row == lax.broadcasted_iota(jnp.int32, (TILE, depth), 0)
    for walker in range(walkers):
        spread = jnp.where(diagonal, repeated[walker : walker + 1, :], 0.0)
        spread_ref[walker * TILE : (walker + 1) * TILE, :] = spread.astype(BF)
    for part in range(rows // TILE):
        right = chol_ref[:, part * TILE : (part + 1) * TILE, :].reshape(depth, orbitals)
        acc_ref[part] += jnp.dot(spread_ref[...], right, preferred_element_type=F32)

    @pl.when(step == pl.num_programs(0) - 1)
    def _():
        parts = rows // TILE
        for part in range(parts):
            for walker in range(walkers):
                place = (walker % planes) * (walkers // planes * parts) + walker // planes * parts + part
                out_ref[place] = acc_ref[part, walker * TILE : (walker + 1) * TILE, :].astype(BF)


def partial_operators(draws, chol_vectors, planes, group=64):
    vectors, rows, orbitals = chol_vectors.shape
    walkers = draws.shape[0]
    parts = rows // TILE
    steps = vectors // group
    blocked = jnp.transpose(draws.reshape(walkers, steps, group), (1, 0, 2))
    return pl.pallas_call(
        functools.partial(operator_kernel, planes),
        grid=(steps,),
        in_specs=[
            pl.BlockSpec((1, walkers, group), lambda i: (i, 0, 0)),
            pl.BlockSpec((group, rows, orbitals), lambda i: (i, 0, 0)),
        ],
        out_specs=pl.BlockSpec((walkers * parts, TILE, orbitals), lambda i: (0, 0, 0)),
        out_shape=jax.ShapeDtypeStruct((walkers * parts, TILE, orbitals), BF),
        scratch_shapes=[
            pltpu.VMEM((parts, walkers * TILE, orbitals), F32),
            pltpu.VMEM((walkers * TILE, group * TILE), BF),
        ],
        compiler_params=pltpu.CompilerParams(vmem_limit_bytes=40 << 20),
        cost_estimate=pl.CostEstimate(
            flops=2 * walkers * TILE * vectors * rows * orbitals,
            bytes_accessed=vectors * rows * orbitals * 2,
            transcendentals=0,
        ),
        name="operators",
    )(blocked, chol_vectors)


def energy_kernel(count, own_ref, other_ref, *refs):
    dual_refs, (out_ref, acc_ref) = refs[:count], refs[count:]
    step = pl.program_id(0)
    half = pl.num_programs(0) // 2
    group, occ, orbitals = own_ref.shape

    @pl.when(step == 0)
    def _():
        acc_ref[...] = jnp.zeros_like(acc_ref)

    def fold(vectors_ref):
        left = vectors_ref[...].reshape(group * occ, orbitals)
        for pair in range(0, count, 2):
            right = jnp.concatenate([dual_refs[pair][...], dual_refs[pair + 1][...]], axis=1)
            products = jnp.dot(left, right, preferred_element_type=F32)
            for member in range(2):
                total = None
                for vector in range(group):
                    block = products[vector * occ : (vector + 1) * occ, member * occ : (member + 1) * occ]
                    term = block * block.T
                    total = term if total is None else total + term
                acc_ref[pair + member] += total.reshape(occ // 8, 8, occ).sum(0)

    pl.when(step < half)(lambda: fold(own_ref))
    pl.when(step >= half)(lambda: fold(other_ref))

    @pl.when(step == pl.num_programs(0) - 1)
    def _():
        out_ref[...] = acc_ref[...]


def energies(own, other, duals, group=8):
    vectors, occ, orbitals = own.shape
    count = len(duals)
    half = vectors // group
    whole = lambda i: (0, 0)
    return pl.pallas_call(
        functools.partial(energy_kernel, count),
        grid=(2 * half,),
        in_specs=[
            pl.BlockSpec((group, occ, orbitals), lambda i: (jnp.minimum(i, half - 1), 0, 0)),
            pl.BlockSpec((group, occ, orbitals), lambda i: (jnp.maximum(i - half, 0), 0, 0)),
        ]
        + [pl.BlockSpec((orbitals, occ), whole)] * count,
        out_specs=pl.BlockSpec((count, 8, occ), lambda i: (0, 0, 0)),
        out_shape=jax.ShapeDtypeStruct((count, 8, occ), F32),
        scratch_shapes=[pltpu.VMEM((count, 8, occ), F32)],
        compiler_params=pltpu.CompilerParams(vmem_limit_bytes=40 << 20),
        cost_estimate=pl.CostEstimate(
            flops=4 * vectors * count * occ * occ * orbitals,
            bytes_accessed=4 * vectors * occ * orbitals,
            transcendentals=0,
        ),
        name="energies",
    )(own, other, *duals)


def flat(chol, z, y, core, walk):
    return chol * walk + (z * 2 + y) * 2 + core


def per_device(field_draws, chol_vectors, rotated_vectors, walkers):
    planes, walk = lax.axis_size("chol"), lax.axis_size("walk")
    depth = walk // 4
    chol, place = lax.axis_index("chol"), lax.axis_index("walk")
    core, z = place % 2, place // 4
    slab_vectors, slab_rows, orbitals = chol_vectors.shape
    occ = walkers.shape[2]
    swap = [(i, i ^ 1) for i in range(walk)]
    every = [(c, zz, y, k) for c in range(2) for zz in range(depth) for y in range(2) for k in range(2)]

    def send(array, target):
        pairs = [(flat(*at, walk), flat(*target(*at), walk)) for at in every if target(*at) is not None]
        return lax.ppermute(array, BOTH, pairs)

    other_vectors = lax.ppermute(rotated_vectors, "walk", swap)
    other_walker = lax.ppermute(walkers, "walk", swap)

    draws = lax.all_to_all(
        jnp.broadcast_to(field_draws, (walk, slab_vectors)), "walk", split_axis=0, concat_axis=0, tiled=True
    )
    partial = partial_operators(draws, chol_vectors, planes)
    pieces = lax.all_to_all(partial, BOTH, split_axis=0, concat_axis=0, tiled=True)
    pieces = pieces.reshape(planes, walk, TILE, orbitals).astype(F32).sum(0).astype(BF)
    other_pieces = lax.ppermute(pieces, "walk", swap)
    first = jnp.where(core == 0, pieces, other_pieces)
    second = jnp.where(core == 0, other_pieces, pieces)
    operators = jnp.stack([first, second], axis=1).reshape(orbitals, orbitals)

    walker = jnp.where(core == chol, walkers[0], other_walker[0])
    propagated = propagate(operators, walker)
    dual = dual_of(walker, propagated)
    across = send(propagated, lambda c, zz, y, k: (1 - c, zz, y, k) if k == c else None)
    propagated = jnp.where(core == chol, propagated, across)[None]

    def along(shift):
        def target(c, zz, y, k):
            if zz // 2 != k:
                return None
            if shift == 0:
                return (c, zz ^ 1, y, k)
            far = (2 * (1 - k)) + ((zz % 2) ^ (shift - 1))
            return (c, far, y, k)

        return target

    near, far_a, far_b = send(dual, along(0)), send(dual, along(1)), send(dual, along(2))
    odd = z % 2 == 1
    inside = z // 2 == core
    even_dual = jnp.where(inside, jnp.where(odd, near, dual), jnp.where(odd, far_b, far_a))
    odd_dual = jnp.where(inside, jnp.where(odd, dual, near), jnp.where(odd, far_a, far_b))
    mine = (even_dual, odd_dual)
    turn = lambda c, zz, y, k: (c, zz, 1 - y, k) if k == 0 else (1 - c, zz, y, k)
    back = lambda c, zz, y, k: (1 - c, zz, y, k) if k == 0 else (c, zz, 1 - y, k)
    one = tuple(send(d, turn) for d in mine)
    terms = [energies(rotated_vectors, other_vectors, mine)]
    two = tuple(send(d, back) for d in mine + one)
    terms.append(energies(rotated_vectors, other_vectors, one))
    terms.append(energies(rotated_vectors, other_vectors, two))
    terms = jnp.concatenate(terms, 0).sum(1)

    y = place // 2 % 2
    slots = []
    for order in range(4):
        first_axis, second_axis = order % 2, order // 2
        y_flip = jnp.where(core == 0, first_axis, second_axis)
        x_flip = jnp.where(core == 0, second_axis, first_axis)
        for parity in range(2):
            slots.append(((2 * core + parity) * 2 + (y ^ y_flip)) * 2 + (chol ^ x_flip))
    slots = jnp.stack(slots)
    hit = (slots[None, :, None] == jnp.arange(walk)[:, None, None]).astype(F32)
    sent = (hit * terms[None]).sum(1)
    sent = jnp.broadcast_to(sent, (planes,) + sent.shape).reshape(planes * walk, occ)
    came = lax.all_to_all(sent, BOTH, split_axis=0, concat_axis=0, tiled=True)
    return propagated, -0.5 * came.sum().reshape(1)


def per_device_plain(field_draws, chol_vectors, rotated_vectors, walkers):
    local_walkers, orbitals, occ = walkers.shape
    total_walkers = local_walkers * lax.axis_size("walk")
    slab_vectors, slab_rows, _ = chol_vectors.shape
    all_draws = lax.all_gather(field_draws, "walk", axis=0, tiled=True)
    partial_rows = jnp.dot(
        all_draws, chol_vectors.reshape(slab_vectors, slab_rows * orbitals), preferred_element_type=F32
    )
    partial_rows = partial_rows.reshape(total_walkers, slab_rows, orbitals)
    summed_rows = lax.psum(partial_rows, "chol").astype(BF)
    operators = lax.all_to_all(summed_rows, "walk", split_axis=0, concat_axis=1, tiled=True)
    propagated = jax.vmap(propagate)(operators, walkers)
    duals = jax.vmap(dual_of)(walkers, propagated)
    dual_cols = jnp.transpose(duals, (1, 0, 2)).reshape(orbitals, local_walkers * occ)
    columns = lax.all_gather(dual_cols, "walk", axis=1, tiled=True)

    def vector_step(vector, summed):
        single = lax.dynamic_index_in_dim(rotated_vectors, vector, 0, keepdims=False)
        tiled = jnp.dot(single, columns, preferred_element_type=F32).reshape(occ, total_walkers, occ)
        return summed + jnp.einsum("iwj,jwi->w", tiled, tiled)

    totals = lax.fori_loop(0, rotated_vectors.shape[0], vector_step, jnp.zeros((total_walkers,), F32))
    summed = lax.psum(totals, BOTH)
    mine = lax.dynamic_slice_in_dim(summed, lax.axis_index("walk") * local_walkers, local_walkers, 0)
    return propagated, -0.5 * mine


def solution(mesh):
    planes, walk = mesh.shape["chol"], mesh.shape["walk"]

    def step(field_draws, chol_vectors, rotated_vectors, walkers):
        rows = chol_vectors.shape[1]
        fits = planes == 2 and walk == 16 and walkers.shape[0] == 1 and rows == 2 * TILE
        body = per_device if fits else per_device_plain
        return body(field_draws, chol_vectors, rotated_vectors, walkers)

    return jax.shard_map(
        step,
        mesh=mesh,
        in_specs=(
            P("walk", "chol"),
            P("chol", "walk", None),
            P(("chol", "walk"), None, None),
            P("walk", None, None),
        ),
        out_specs=(P("walk", None, None), P("walk")),
        check_vma=False,
    )
```

time: 481 us -> 175 us (0.36)
  matrix products: 177 us -> 3.13 us
  blocking collectives: 109 us -> 13.5 us
  local copies, waits for them, and re-layouts: 97.2 us -> 4.89 us
  Pallas kernels: 0 us -> 67.4 us
  starting transfers between devices: 0.04 us -> 29.5 us
  waiting for transfers between devices: 40 us -> 26 us
  between operations: 15.9 us -> 2.84 us
  other arithmetic: 37.7 us -> 26.3 us
    dot_general x70 -> x5, matrix products: 175 us -> 1.48 us  [the longest x4 1.17 us: propagate(): applied = jnp.dot(operators, taylor_term, preferred_element_type=F32)]
    psum x2 -> x0, blocking collectives: 68.4 us -> none  [the longest x1 38.3 us: per_device(): summed = lax.psum(totals, ('chol', 'walk'))]
    pallas_call x0 -> x4, Pallas kernels: none -> 67.4 us  [the longest x3 45.4 us: energies(): pl.pallas_call(functools.partial(energy_kernel, count), grid=(2 * half,),...]
    dot_general x1 -> x0, local copies, waits for them, and re-layouts: 44 us -> none  [per_device(): jnp.dot(all_draws, chol_vectors.reshape(slab_vectors, slab_rows * orbital...]
    all_gather x1 -> x0, waiting for transfers between devices: 39.9 us -> none  [per_device(): lax.all_gather(dual_cols, 'walk', axis=1, tiled=True)]
    unnamed x7 -> x6, local copies, waits for them, and re-layouts: 31 us -> 3.43 us
    all_gather x1 -> x0, blocking collectives: 23.2 us -> none  [per_device(): all_draws = lax.all_gather(field_draws, 'walk', axis=0, tiled=True)]
    all_to_all x0 -> x2, waiting for transfers between devices: none -> 22 us  [the longest x1 15.6 us: per_device(): lax.all_to_all(partial, BOTH, split_axis=0, concat_axis=0, tiled=True)]
  transfers between devices with their start and end apart: 1 -> 15, of which waited for: 1 -> 7; matrix products, arithmetic and copies ran while one was open for 0% -> 17% of each run, Pallas kernels for 0% -> 39%
where the time goes in v1:
time: 175 us; the launch traced here: 174 us
  Pallas kernels  67.4 us (39%)
  starting transfers between devices  29.5 us (17%)
  other arithmetic  26.3 us (15%)
  waiting for transfers between devices  26 us (15%)
  blocking collectives  13.5 us (8%)
  local copies, waits for them, and re-layouts  4.89 us (3%)
  matrix products  3.13 us (2%)
  between operations  2.84 us (2%)
    pallas_call x3, Pallas kernels, energies(): pl.pallas_call(functools.partial(energy_kernel, count), grid=(2 * half,),...  45.4 us
    pallas_call x1, Pallas kernels, partial_operators(): pl.pallas_call(functools.partial(operator_kernel, planes), grid=(steps,),...  22 us
    all_to_all x1, waiting for transfers between devices, per_device(): lax.all_to_all(partial, BOTH, split_axis=0, concat_axis=0, tiled=True)  15.6 us
    ppermute x10, starting transfers between devices, send(): return lax.ppermute(array, BOTH, pairs)  14.7 us
    all_to_all x1, blocking collectives, per_device(): lax.all_to_all(jnp.broadcast_to(field_draws, (walk, slab_vectors)), 'walk...  13.5 us
    another operation x3, other arithmetic, solve_dual(): factor = jnp.linalg.cholesky(gram)  12.4 us
    another operation x2, other arithmetic, solve_dual(): return jax.scipy.linalg.cho_solve((factor, True), right)  10.5 us
    all_to_all x1, starting transfers between devices, per_device(): came = lax.all_to_all(sent, BOTH, split_axis=0, concat_axis=0, tiled=True)  9.53 us
  transfers between devices with their start and end apart: 15, of which 7 were waited for; matrix products, arithmetic and copies ran while one was open for 17% of the time, Pallas kernels for 39%

profile of v1, /device:TPU:0, one launch (start us, length us, event | category | flops | bytes accessed | tf_op | source)
XLA Modules:
  0.0 173.5 jit_solution(7550029409204101658)
XLA Ops:
  0.6 0.5 collective-permute-start.3
  1.1 0.7 reduce.8
  1.9 0.5 broadcast.104
  2.4 0.8 reduce.10
  3.3 13.5 %all_to_all.20 = bf16[16,2,512]{2,1,0:T(2,128)(2,1)S(1)} all-to-all(bf16[16,2,512]{2,1,0:T(2,128)(2,1)S(1)} %reshape.73), channel_id=1, replica_groups=mesh['chol'=2,'walk'=16] {'walk'}, dimensions={0} | all-to-all | bytes 65536 | tf_op jit(solution)/shard_map/all_to_all | solution.py:177
  17.1 22.0 %operators.1 = bf16[32,16,512]{2,1,0:T(8,128)(2,1)} custom-call(bf16[16,16,64]{2,1,0:T(8,128)(2,1)S(1)} %bitcast.54, bf16[1024,32,512]{2,1,0:T(8,128)(2,1)} %chol_ref.1), custom_call_target="tpu_custom_call" | custom-call | flops 8589934592 | bytes 33554432 | tf_op jit(solution)/shard_map/operators/pallas_call | solution.py:76
  39.1 4.4 %all-to-all-start.1 = ((bf16[32,16,512]{2,1,0:T(8,128)(2,1)}), bf16[32,16,512]{2,1,0:T(8,128)(2,1)S(1)}, u32[]{:S(2)}, u32[]{:S(2)}) async-start(bf16[32,16,512]{2,1,0:T(8,128)(2,1)} %operators.1), calls=%async_computation.1 | async-start | bytes 1048576 | tf_op jit(solution)/shard_map/all_to_all | solution.py:181
  43.8 15.6 %all-to-all-done.1 = bf16[32,16,512]{2,1,0:T(8,128)(2,1)S(1)} async-done(((bf16[32,16,512]{2,1,0:T(8,128)(2,1)}), bf16[32,16,512]{2,1,0:T(8,128)(2,1)S(1)}, u32[]{:S(2)}, u32[]{:S(2)}) %all-to-all-start.1) | async-done | bytes 524320 | tf_op jit(solution)/shard_map/all_to_all | solution.py:181
  59.7 1.5 collective-permute-done.1
  63.1 11.7 %cholesky.16 = f32[128,128]{1,0:T(8,128)S(1)} custom-call(f32[128,128]{1,0:T(8,128)S(1)} %fusion.12), custom_call_target="Cholesky" | custom-call | tf_op jit(solution)/shard_map/jit(cholesky)/cholesky | solution.py:19
  74.9 0.6 compare_reduce_fusion
  75.5 0.7 fusion.8
  76.2 9.8 %custom-call.10 = f32[1,128,128]{1,2,0:T(8,128)S(1)} custom-call(f32[1,128,128]{2,1,0:T(8,128)S(1)} %fusion.8), custom_call_target="InvertDiagBlocksLowerTriangular" | custom-call | tf_op jit(solution)/shard_map/jit(_cho_solve)/triangular_solve | solution.py:21
  86.8 0.6 convolution_convert_fusion.1
  87.4 2.5 %collective-permute-start.4 = (bf16[512,128]{1,0:T(8,128)(2,1)S(1)}, bf16[512,128]{1,0:T(8,128)(2,1)S(1)}, u32[]{:S(2)}, u32[]{:S(2)}) collective-permute-start(bf16[512,128]{1,0:T(8,128)(2,1)S(1)} %convolution_convert_fusion.1), channel_id=1, source_target_pairs={{0,4},{2,6},{4,0},{6,2},{9,13},{11,15},{13,9},{15,11},{16,20},{18,... | collective-permute-start | bytes 393224 | tf_op jit(solution)/shard_map/ppermute | solution.py:172
  89.9 2.0 %collective-permute-start.5 = (bf16[512,128]{1,0:T(8,128)(2,1)S(1)}, bf16[512,128]{1,0:T(8,128)(2,1)S(1)}, u32[]{:S(2)}, u32[]{:S(2)}) collective-permute-start(bf16[512,128]{1,0:T(8,128)(2,1)S(1)} %convolution_convert_fusion.1), channel_id=1, source_target_pairs={{0,12},{2,14},{4,8},{6,10},{9,5},{11,7},{13,1},{15,3},{16,28},{18,... | collective-permute-start | bytes 393224 | tf_op jit(solution)/shard_map/ppermute | solution.py:172
  92.0 1.3 collective-permute-start.6
  93.4 0.8 collective-permute-done.4
  94.5 1.4 collective-permute-done.6
  96.3 1.7 collective-permute-start.8
  98.0 2.7 %collective-permute-start.2 = (f32[512,128]{1,0:T(8,128)S(1)}, f32[512,128]{1,0:T(8,128)S(1)}, u32[]{:S(2)}, u32[]{:S(2)}) collective-permute-start(f32[512,128]{1,0:T(8,128)S(1)} %fusion.4), channel_id=1, source_target_pairs={{0,16},{2,18},{4,20},{6,22},{8,24},{10,26},{12,28},{14,30},{17,1},... | collective-permute-start | bytes 786440 | tf_op jit(solution)/shard_map/ppermute | solution.py:172
  100.9 1.9 %collective-permute-start.9 = (bf16[512,128]{1,0:T(8,128)(2,1)S(1)}, bf16[512,128]{1,0:T(8,128)(2,1)S(1)}, u32[]{:S(2)}, u32[]{:S(2)}) collective-permute-start(bf16[512,128]{1,0:T(8,128)(2,1)S(1)} %get-tuple-element.3.refs_0_), channel_id=1, source_target_pairs={{0,16},{1,3},{2,18},{3,1},{4,20},{5,7},{6,22},{7,5},{8,24},{9,11},... | collective-permute-start | bytes 393224 | tf_op jit(solution)/shard_map/ppermute | solution.py:172
  103.0 1.9 %collective-permute-start.12 = (bf16[512,128]{1,0:T(8,128)(2,1)S(1)}, bf16[512,128]{1,0:T(8,128)(2,1)S(1)}, u32[]{:S(2)}, u32[]{:S(2)}) collective-permute-start(bf16[512,128]{1,0:T(8,128)(2,1)S(1)} %collective-permute-done.8.refs_1_), channel_id=1, source_target_pairs={{0,16},{1,3},{2,18},{3,1},{4,20},{5,7},{6,22},{7,5},{8,24},{9,11},... | collective-permute-start | bytes 393224 | tf_op jit(solution)/shard_map/ppermute | solution.py:172
  104.9 3.4 %copy-done = bf16[64,128,512]{2,1,0:T(8,128)(2,1)S(1)} copy-done((bf16[64,128,512]{2,1,0:T(8,128)(2,1)S(1)}, bf16[64,128,512]{2,1,0:T(8,128)(2,1)}, u32[]{:S(2)}) %copy-start) | copy-done | bytes 8388632
  108.3 13.0 %energies.3 = f32[2,8,128]{2,1,0:T(8,128)S(1)} custom-call(bf16[64,128,512]{2,1,0:T(8,128)(2,1)S(1)} %copy-done, bf16[64,128,512]{2,1,0:T(8,128)(2,1)} %collective-permute-done.3.other_ref, bf16[512,128]{1,0:T(8,128)(2,1)S(1)} %get-tuple-element.3.refs_0_, bf16[512,128]{1,0:T(8,128)(2,1)S(1)} %get-tuple-element.2.refs_1_), custom_call_target="tpu_custom_call" | custom-call | flops 4294967296 | bytes 16777216 | tf_op jit(solution)/shard_map/energies/pallas_call | solution.py:135
  121.3 19.4 %energies.5 = f32[4,8,128]{2,1,0:T(8,128)S(1)} custom-call(bf16[64,128,512]{2,1,0:T(8,128)(2,1)S(1)} %copy-done, bf16[64,128,512]{2,1,0:T(8,128)(2,1)} %collective-permute-done.3.other_ref, bf16[512,128]{1,0:T(8,128)(2,1)S(1)} %collective-permute-done.9.refs_0_, bf16[512,128]{1,0:T(8,128)(2,1)S(1)} %collective-permute-done.10.refs_1_, ...), custom_call_target="tpu_custom_call" | custom-call | flops 8589934592 | bytes 16777216 | tf_op jit(solution)/shard_map/energies/pallas_call | solution.py:135
  140.7 13.0 %energies.4 = f32[2,8,128]{2,1,0:T(8,128)S(1)} custom-call(bf16[64,128,512]{2,1,0:T(8,128)(2,1)S(1)} %copy-done, bf16[64,128,512]{2,1,0:T(8,128)(2,1)} %collective-permute-done.3.other_ref, bf16[512,128]{1,0:T(8,128)(2,1)S(1)} %collective-permute-done.7.refs_0_, bf16[512,128]{1,0:T(8,128)(2,1)S(1)} %collective-permute-done.8.refs_1_), custom_call_target="tpu_custom_call" | custom-call | flops 4294967296 | bytes 16777216 | tf_op jit(solution)/shard_map/energies/pallas_call | solution.py:135
  153.8 0.6 broadcast_in_dim.18
  154.4 9.5 %all-to-all-start.2 = ((f32[32,1,128]{2,1,0:T(1,128)}), f32[32,1,128]{2,1,0:T(1,128)S(1)}, u32[]{:S(2)}, u32[]{:S(2)}) async-start(f32[32,1,128]{2,1,0:T(1,128)} %bitcast.19), calls=%async_computation.2 | async-start | bytes 32768 | tf_op jit(solution)/shard_map/all_to_all | solution.py:232
  164.0 0.7 select_bitcast_fusion
  164.7 6.4 %all-to-all-done.2 = f32[32,1,128]{2,1,0:T(1,128)S(1)} async-done(((f32[32,1,128]{2,1,0:T(1,128)}), f32[32,1,128]{2,1,0:T(1,128)S(1)}, u32[]{:S(2)}, u32[]{:S(2)}) %all-to-all-start.2) | async-done | bytes 16416 | tf_op jit(solution)/shard_map/all_to_all | solution.py:232
  171.1 0.6 reduce_sum.42
  (44 shorter events, 4.8 us)
Async XLA Ops:
  0.6 102.4 %collective-permute-start.3 = (bf16[64,128,512]{2,1,0:T(8,128)(2,1)}, bf16[64,128,512]{2,1,0:T(8,128)(2,1)}, u32[]{:S(2)}, u32[]{:S(2)}) collective-permute-start(bf16[64,128,512]{2,1,0:T(8,128)(2,1)} %own_ref.5), channel_id=1, source_target_pairs={{0,1},{1,0},{2,3},{3,2},{4,5},{5,4},{6,7},{7,6},{8,9},{9,8},{10,11... | collective-permute-start | bytes 25165832 | tf_op jit(solution)/shard_map/ppermute | solution.py:174
  17.1 26.4 %copy-start.1 = (bf16[1,512,128]{2,1,0:T(8,128)(2,1)S(1)}, bf16[1,512,128]{2,1,0:T(8,128)(2,1)}, u32[]{:S(2)}) copy-start(bf16[1,512,128]{2,1,0:T(8,128)(2,1)} %param.7) | copy-start | bytes 393220
  39.1 20.3 %all-to-all-start.1 = ((bf16[32,16,512]{2,1,0:T(8,128)(2,1)}), bf16[32,16,512]{2,1,0:T(8,128)(2,1)S(1)}, u32[]{:S(2)}, u32[]{:S(2)}) async-start(bf16[32,16,512]{2,1,0:T(8,128)(2,1)} %operators.1), calls=%async_computation.1 | async-start | bytes 1048576 | tf_op jit(solution)/shard_map/all_to_all | solution.py:181
  43.5 16.1 %collective-permute-start = (bf16[1,512,128]{2,1,0:T(8,128)(2,1)S(1)}, bf16[1,512,128]{2,1,0:T(8,128)(2,1)S(1)}, u32[]{:S(2)}, u32[]{:S(2)}) collective-permute-start(bf16[1,512,128]{2,1,0:T(8,128)(2,1)S(1)} %copy-done.1), channel_id=1, source_target_pairs={{0,1},{1,0},{2,3},{3,2},{4,5},{5,4},{6,7},{7,6},{8,9},{9,8},{10,11... | collective-permute-start | bytes 393224 | tf_op jit(solution)/shard_map/ppermute | solution.py:175
  59.5 1.6 collective-permute-start.1
  87.4 6.9 %collective-permute-start.4 = (bf16[512,128]{1,0:T(8,128)(2,1)S(1)}, bf16[512,128]{1,0:T(8,128)(2,1)S(1)}, u32[]{:S(2)}, u32[]{:S(2)}) collective-permute-start(bf16[512,128]{1,0:T(8,128)(2,1)S(1)} %convolution_convert_fusion.1), channel_id=1, source_target_pairs={{0,4},{2,6},{4,0},{6,2},{9,13},{11,15},{13,9},{15,11},{16,20},{18,... | collective-permute-start | bytes 393224 | tf_op jit(solution)/shard_map/ppermute | solution.py:172
  89.9 4.6 %collective-permute-start.5 = (bf16[512,128]{1,0:T(8,128)(2,1)S(1)}, bf16[512,128]{1,0:T(8,128)(2,1)S(1)}, u32[]{:S(2)}, u32[]{:S(2)}) collective-permute-start(bf16[512,128]{1,0:T(8,128)(2,1)S(1)} %convolution_convert_fusion.1), channel_id=1, source_target_pairs={{0,12},{2,14},{4,8},{6,10},{9,5},{11,7},{13,1},{15,3},{16,28},{18,... | collective-permute-start | bytes 393224 | tf_op jit(solution)/shard_map/ppermute | solution.py:172
  92.0 3.9 %collective-permute-start.6 = (bf16[512,128]{1,0:T(8,128)(2,1)S(1)}, bf16[512,128]{1,0:T(8,128)(2,1)S(1)}, u32[]{:S(2)}, u32[]{:S(2)}) collective-permute-start(bf16[512,128]{1,0:T(8,128)(2,1)S(1)} %convolution_convert_fusion.1), channel_id=1, source_target_pairs={{0,8},{2,10},{4,12},{6,14},{9,1},{11,3},{13,5},{15,7},{16,24},{18,... | collective-permute-start | bytes 393224 | tf_op jit(solution)/shard_map/ppermute | solution.py:172
  95.9 5.0 %collective-permute-start.7 = (bf16[512,128]{1,0:T(8,128)(2,1)S(1)}, bf16[512,128]{1,0:T(8,128)(2,1)S(1)}, u32[]{:S(2)}, u32[]{:S(2)}) collective-permute-start(bf16[512,128]{1,0:T(8,128)(2,1)S(1)} %get-tuple-element.3.refs_0_), channel_id=1, source_target_pairs={{0,2},{1,17},{2,0},{3,19},{4,6},{5,21},{6,4},{7,23},{8,10},{9,25},... | collective-permute-start | bytes 393224 | tf_op jit(solution)/shard_map/ppermute | solution.py:172
  96.3 6.6 %collective-permute-start.8 = (bf16[512,128]{1,0:T(8,128)(2,1)S(1)}, bf16[512,128]{1,0:T(8,128)(2,1)S(1)}, u32[]{:S(2)}, u32[]{:S(2)}) collective-permute-start(bf16[512,128]{1,0:T(8,128)(2,1)S(1)} %get-tuple-element.2.refs_1_), channel_id=1, source_target_pairs={{0,2},{1,17},{2,0},{3,19},{4,6},{5,21},{6,4},{7,23},{8,10},{9,25},... | collective-permute-start | bytes 393224 | tf_op jit(solution)/shard_map/ppermute | solution.py:172
  98.0 66.0 %collective-permute-start.2 = (f32[512,128]{1,0:T(8,128)S(1)}, f32[512,128]{1,0:T(8,128)S(1)}, u32[]{:S(2)}, u32[]{:S(2)}) collective-permute-start(f32[512,128]{1,0:T(8,128)S(1)} %fusion.4), channel_id=1, source_target_pairs={{0,16},{2,18},{4,20},{6,22},{8,24},{10,26},{12,28},{14,30},{17,1},... | collective-permute-start | bytes 786440 | tf_op jit(solution)/shard_map/ppermute | solution.py:172
  100.7 20.5 %collective-permute-start.10 = (bf16[512,128]{1,0:T(8,128)(2,1)S(1)}, bf16[512,128]{1,0:T(8,128)(2,1)S(1)}, u32[]{:S(2)}, u32[]{:S(2)}) collective-permute-start(bf16[512,128]{1,0:T(8,128)(2,1)S(1)} %get-tuple-element.2.refs_1_), channel_id=1, source_target_pairs={{0,16},{1,3},{2,18},{3,1},{4,20},{5,7},{6,22},{7,5},{8,24},{9,11},... | collective-permute-start | bytes 393224 | tf_op jit(solution)/shard_map/ppermute | solution.py:172
  100.9 20.3 %collective-permute-start.9 = (bf16[512,128]{1,0:T(8,128)(2,1)S(1)}, bf16[512,128]{1,0:T(8,128)(2,1)S(1)}, u32[]{:S(2)}, u32[]{:S(2)}) collective-permute-start(bf16[512,128]{1,0:T(8,128)(2,1)S(1)} %get-tuple-element.3.refs_0_), channel_id=1, source_target_pairs={{0,16},{1,3},{2,18},{3,1},{4,20},{5,7},{6,22},{7,5},{8,24},{9,11},... | collective-permute-start | bytes 393224 | tf_op jit(solution)/shard_map/ppermute | solution.py:172
  102.8 18.4 %collective-permute-start.11 = (bf16[512,128]{1,0:T(8,128)(2,1)S(1)}, bf16[512,128]{1,0:T(8,128)(2,1)S(1)}, u32[]{:S(2)}, u32[]{:S(2)}) collective-permute-start(bf16[512,128]{1,0:T(8,128)(2,1)S(1)} %collective-permute-done.7.refs_0_), channel_id=1, source_target_pairs={{0,16},{1,3},{2,18},{3,1},{4,20},{5,7},{6,22},{7,5},{8,24},{9,11},... | collective-permute-start | bytes 393224 | tf_op jit(solution)/shard_map/ppermute | solution.py:172
  103.0 18.3 %collective-permute-start.12 = (bf16[512,128]{1,0:T(8,128)(2,1)S(1)}, bf16[512,128]{1,0:T(8,128)(2,1)S(1)}, u32[]{:S(2)}, u32[]{:S(2)}) collective-permute-start(bf16[512,128]{1,0:T(8,128)(2,1)S(1)} %collective-permute-done.8.refs_1_), channel_id=1, source_target_pairs={{0,16},{1,3},{2,18},{3,1},{4,20},{5,7},{6,22},{7,5},{8,24},{9,11},... | collective-permute-start | bytes 393224 | tf_op jit(solution)/shard_map/ppermute | solution.py:172
  104.9 3.4 %copy-start = (bf16[64,128,512]{2,1,0:T(8,128)(2,1)S(1)}, bf16[64,128,512]{2,1,0:T(8,128)(2,1)}, u32[]{:S(2)}) copy-start(bf16[64,128,512]{2,1,0:T(8,128)(2,1)} %own_ref.5) | copy-start | bytes 25165828
  154.4 16.7 %all-to-all-start.2 = ((f32[32,1,128]{2,1,0:T(1,128)}), f32[32,1,128]{2,1,0:T(1,128)S(1)}, u32[]{:S(2)}, u32[]{:S(2)}) async-start(f32[32,1,128]{2,1,0:T(1,128)} %bitcast.19), calls=%async_computation.2 | async-start | bytes 32768 | tf_op jit(solution)/shard_map/all_to_all | solution.py:232

commit v2 on v1

v2 whole, which is shorter than its diff:
```python
import functools

import jax
import jax.numpy as jnp
from jax import lax
from jax.experimental import pallas as pl
from jax.experimental.pallas import tpu as pltpu
from jax.sharding import PartitionSpec as P

TERMS = 4
TILE = 16
GROUPS = 4
BF = jnp.bfloat16
F32 = jnp.float32
BOTH = ("chol", "walk")


def in_hbm(array):
    return pltpu.with_memory_space_constraint(array, pltpu.HBM)


def in_vmem(array):
    return pltpu.with_memory_space_constraint(array, pltpu.VMEM)


def solve_dual(correlation, transposed):
    gram = jnp.dot(correlation, correlation.T, precision=lax.Precision.HIGHEST)
    factor = jnp.linalg.cholesky(gram)
    right = jnp.dot(correlation, transposed, precision=lax.Precision.HIGHEST)
    return jax.scipy.linalg.cho_solve((factor, True), right)


def propagate(operators, walkers):
    taylor_term = walkers
    propagated = walkers.astype(F32)
    for degree in range(1, TERMS + 1):
        applied = jnp.dot(operators, taylor_term, preferred_element_type=F32)
        taylor_term = (applied / degree).astype(BF)
        propagated = propagated + taylor_term.astype(F32)
    return propagated


def dual_of(walkers, propagated):
    correlation = jnp.dot(walkers.astype(F32).T, propagated, precision=lax.Precision.HIGHEST)
    return solve_dual(correlation, propagated.T).T.astype(BF)


def operator_kernel(planes, draws_ref, chol_ref, out_ref, near_ref, far_ref, repeat_ref, spread_ref, sums_ref, sems):
    walkers, steps, group = draws_ref.shape
    rows, orbitals = chol_ref.shape[1:]
    wide = orbitals // GROUPS
    depth = group * TILE
    parts = rows // TILE
    own_group = lax.axis_index("walk") * rows // wide
    upper = jnp.where(own_group >= GROUPS // 2, 1, 0)

    def columns(shift):
        return pl.ds(pl.multiple_of((own_group + shift) % GROUPS * wide, wide), wide)

    copies = []
    for step in range(steps):
        whole, half = pl.ds(step * group, group), pl.ds(step * group + upper * (group // 2), group // 2)
        pairs = [
            (chol_ref.at[whole, :, columns(0)], near_ref.at[step, :, :, pl.ds(0, wide)]),
            (chol_ref.at[whole, :, columns(1)], near_ref.at[step, :, :, pl.ds(wide, wide)]),
            (chol_ref.at[half, :, columns(2)], far_ref.at[step]),
        ]
        copies.append([pltpu.make_async_copy(*pair, sems.at[step, at]) for at, pair in enumerate(pairs)])
        for copy in copies[-1]:
            copy.start()

    owner = lax.broadcasted_iota(jnp.int32, (group, depth), 1) // TILE
    mine = owner == lax.broadcasted_iota(jnp.int32, (group, depth), 0)
    repeat_ref[...] = jnp.where(mine, 1.0, 0.0).astype(BF)
    lane_row = lax.broadcasted_iota(jnp.int32, (TILE, depth), 1) % TILE
    diagonal = lane_row == lax.broadcasted_iota(jnp.int32, (TILE, depth), 0)
    draws = draws_ref[...].astype(F32)

    def spread(step):
        repeated = jnp.dot(draws[:, step, :].astype(BF), repeat_ref[...], preferred_element_type=F32)
        for walker in range(walkers):
            block = jnp.where(diagonal, repeated[walker : walker + 1, :], 0.0)
            spread_ref[step % 2, walker * TILE : (walker + 1) * TILE, :] = block.astype(BF)

    def add(at, step, value):
        sums_ref[at] = value if step == 0 else sums_ref[at] + value

    spread(0)
    half_lanes = pl.ds(pl.multiple_of(upper * (depth // 2), depth // 2), depth // 2)
    for step in range(steps):
        if step + 1 < steps:
            spread(step + 1)
        for copy in copies[step]:
            copy.wait()
        far = []
        for part in range(parts):
            taken = slice(part * TILE, (part + 1) * TILE)
            right = near_ref[step, :, taken, :].reshape(depth, 2 * wide)
            add(part, step, jnp.dot(spread_ref[step % 2], right, preferred_element_type=F32))
            far.append(far_ref[step, :, taken, :].reshape(depth // 2, wide))
        right = jnp.concatenate(far, axis=1)
        add(parts, step, jnp.dot(spread_ref[step % 2, :, half_lanes], right, preferred_element_type=F32))

    for part in range(parts):
        for walker in range(walkers):
            place = (walker % planes) * (walkers // planes * parts) + walker // planes * parts + part
            taken = slice(walker * TILE, (walker + 1) * TILE)
            out_ref[place, :, : 2 * wide] = sums_ref[part, taken, :].astype(BF)
            out_ref[place, :, 2 * wide :] = sums_ref[parts, taken, part * wide : (part + 1) * wide].astype(BF)


def partial_operators(draws, chol_vectors, planes):
    walkers, steps, group = draws.shape
    vectors, rows, orbitals = chol_vectors.shape
    parts, wide = rows // TILE, orbitals // GROUPS
    vmem = pl.BlockSpec(memory_space=pltpu.VMEM)
    return pl.pallas_call(
        functools.partial(operator_kernel, planes),
        in_specs=[vmem, pl.BlockSpec(memory_space=pl.ANY)],
        out_specs=vmem,
        out_shape=jax.ShapeDtypeStruct((walkers * parts, TILE, 3 * wide), BF),
        scratch_shapes=[
            pltpu.VMEM((steps, group, rows, 2 * wide), BF),
            pltpu.VMEM((steps, group // 2, rows, wide), BF),
            pltpu.VMEM((group, group * TILE), BF),
            pltpu.VMEM((2, walkers * TILE, group * TILE), BF),
            pltpu.VMEM((parts + 1, walkers * TILE, 2 * wide), F32),
            pltpu.SemaphoreType.DMA((steps, 3)),
        ],
        compiler_params=pltpu.CompilerParams(vmem_limit_bytes=32 << 20),
        cost_estimate=pl.CostEstimate(
            flops=10 * walkers * TILE * vectors * rows * wide // 2,
            bytes_accessed=vectors * rows * wide * 5,
            transcendentals=0,
        ),
        name="operators",
    )(draws, in_hbm(chol_vectors))


def pieces_of(value, count):
    found = []
    for _ in range(count):
        piece = value.astype(BF)
        found.append(piece)
        value = value - piece.astype(F32)
    return found


def fine_dot(a, b):
    left = jnp.concatenate([a[0], a[0], a[1]], axis=1)
    right = jnp.concatenate([b[0], b[1], b[0]], axis=0)
    return jnp.dot(left, right, preferred_element_type=F32)


def full_dot(a, b):
    return jnp.dot(a, b, precision=lax.Precision.HIGHEST, preferred_element_type=F32)


def inverse_of(matrix):
    size = matrix.shape[0]
    shape = (size, size)
    one = jnp.where(lax.broadcasted_iota(jnp.int32, shape, 0) == lax.broadcasted_iota(jnp.int32, shape, 1), 1.0, 0.0)
    largest = jnp.max(jnp.sum(jnp.abs(matrix), axis=1, keepdims=True), axis=0, keepdims=True)
    guess = one * (1.5 / largest)
    halves = pieces_of(matrix, 2)

    def rough(carry):
        count, _, x = carry
        for _ in range(3):
            rest = one - fine_dot(halves, pieces_of(x, 2))
            x = x + fine_dot(pieces_of(x, 2), pieces_of(rest, 2))
        return count + 1, jnp.sum(rest * rest), x

    def exact(carry):
        count, _, x = carry
        rest = one - full_dot(matrix, x)
        return count + 1, jnp.sum(rest * rest), x + full_dot(x, rest)

    _, _, guess = lax.while_loop(
        lambda c: jnp.logical_and(c[0] < 14, c[1] > 1e-4), rough, (jnp.int32(0), jnp.float32(1), guess)
    )
    _, _, guess = lax.while_loop(
        lambda c: jnp.logical_and(c[0] < 6, c[1] > 1e-6), exact, (jnp.int32(0), jnp.float32(1), guess)
    )
    return guess


def solve_kernel(
    planes,
    own_rows_ref,
    other_rows_ref,
    own_walker_ref,
    other_walker_ref,
    own_ref,
    other_ref,
    propagated_ref,
    dual_ref,
    own_out_ref,
    other_out_ref,
    rows_ref,
    operators_ref,
    own_sem,
    other_sem,
):
    own_copy = pltpu.make_async_copy(own_ref, own_out_ref, own_sem)
    other_copy = pltpu.make_async_copy(other_ref, other_out_ref, other_sem)
    own_copy.start()
    other_copy.start()
    core, chol = lax.axis_index("walk") % 2, lax.axis_index("chol")
    slabs, wide = own_rows_ref.shape[0] // planes, own_rows_ref.shape[2] // 3
    for slab in range(slabs):
        for from_ref, side in ((own_rows_ref, core), (other_rows_ref, 1 - core)):
            summed = from_ref[slab].astype(F32)
            for plane in range(1, planes):
                summed = summed + from_ref[plane * slabs + slab].astype(F32)
            rows_ref[pl.ds(pl.multiple_of((2 * slab + side) * TILE, TILE), TILE), :] = summed
    group = lambda k: slice(k % GROUPS * wide, (k % GROUPS + 1) * wide)
    for k in range(GROUPS):
        operators_ref[group(k), group(k)] = rows_ref[group(k), group(0)].astype(BF)
        after = rows_ref[group(k), group(1)]
        operators_ref[group(k), group(k + 1)] = after.astype(BF)
        operators_ref[group(k + 1), group(k)] = after.T.astype(BF)
    for k in range(GROUPS // 2):
        one, two = rows_ref[group(k), group(2)], rows_ref[group(k + 2), group(2)]
        operators_ref[group(k), group(k + 2)] = (one + two.T).astype(BF)
        operators_ref[group(k + 2), group(k)] = (one.T + two).astype(BF)
    mine = jnp.where(core == chol, 1.0, 0.0)
    walker = own_walker_ref[...].astype(F32) * mine + other_walker_ref[...].astype(F32) * (1.0 - mine)
    taylor_term = walker.astype(BF)
    transposed = taylor_term.T
    propagated = walker
    for degree in range(1, TERMS + 1):
        applied = jnp.dot(operators_ref[...], taylor_term, preferred_element_type=F32)
        taylor_term = (applied / degree).astype(BF)
        propagated = propagated + taylor_term.astype(F32)
    propagated_ref[...] = propagated
    correlation = None
    for piece in pieces_of(propagated, 3):
        part = jnp.dot(transposed, piece, preferred_element_type=F32)
        correlation = part if correlation is None else correlation + part
    dual_ref[...] = full_dot(propagated, inverse_of(correlation)).astype(BF)
    own_copy.wait()
    other_copy.wait()


def solve(own_rows, other_rows, own_walker, other_walker, own, other, planes):
    orbitals = own_walker.shape[0]
    vmem, anywhere = pl.BlockSpec(memory_space=pltpu.VMEM), pl.BlockSpec(memory_space=pl.ANY)
    return pl.pallas_call(
        functools.partial(solve_kernel, planes),
        in_specs=[vmem] * 4 + [anywhere] * 2,
        out_specs=[vmem] * 4,
        out_shape=[
            jax.ShapeDtypeStruct(own_walker.shape, F32),
            jax.ShapeDtypeStruct(own_walker.shape, BF),
            pltpu.VMEM(own.shape, BF),
            pltpu.VMEM(other.shape, BF),
        ],
        scratch_shapes=[
            pltpu.VMEM((orbitals, own_rows.shape[2]), F32),
            pltpu.VMEM((orbitals, orbitals), BF),
            pltpu.SemaphoreType.DMA,
            pltpu.SemaphoreType.DMA,
        ],
        compiler_params=pltpu.CompilerParams(vmem_limit_bytes=16 << 20),
        cost_estimate=pl.CostEstimate(flops=6 * 10**9, bytes_accessed=16 << 20, transcendentals=0),
        name="solve",
    )(own_rows, other_rows, own_walker, other_walker, in_hbm(own), in_hbm(other))


def energy_kernel(group, sub, own_ref, other_ref, *refs):
    dual_refs, out_ref = refs[:-1], refs[-1]
    vectors, occ, orbitals = own_ref.shape
    pairs = [jnp.concatenate([ref[0], ref[1]], axis=1) for ref in dual_refs]
    count = 2 * len(pairs)
    out_ref[...] = jnp.zeros_like(out_ref)
    for vectors_ref in (own_ref, other_ref):

        @pl.loop(0, vectors, step=group)
        def _(start):
            totals = [None] * count
            for at in range(0, group, sub):
                left = vectors_ref[pl.ds(start + at, sub)].reshape(sub * occ, orbitals)
                for pair, right in enumerate(pairs):
                    products = jnp.dot(left, right, preferred_element_type=F32)
                    for member in range(2):
                        for vector in range(sub):
                            block = products[vector * occ : (vector + 1) * occ, member * occ : (member + 1) * occ]
                            term = (block * block.T).reshape(occ // 8, 8, occ).sum(0)
                            slot = 2 * pair + member
                            totals[slot] = term if totals[slot] is None else totals[slot] + term
            for slot in range(count):
                out_ref[slot] += totals[slot]


def energies(own, other, duals, group=32, sub=2):
    vectors, occ, orbitals = own.shape
    count = 2 * len(duals)
    vmem = pl.BlockSpec(memory_space=pltpu.VMEM)
    return pl.pallas_call(
        functools.partial(energy_kernel, group, sub),
        in_specs=[vmem] * (2 + len(duals)),
        out_specs=vmem,
        out_shape=jax.ShapeDtypeStruct((count, 8, occ), F32),
        compiler_params=pltpu.CompilerParams(vmem_limit_bytes=16 << 20),
        cost_estimate=pl.CostEstimate(
            flops=4 * vectors * count * occ * occ * orbitals,
            bytes_accessed=4 * vectors * occ * orbitals,
            transcendentals=0,
        ),
        name="energies",
    )(in_vmem(own), in_vmem(other), *duals)


def flat(chol, z, y, core, walk):
    return chol * walk + (z * 2 + y) * 2 + core


def per_device(field_draws, chol_vectors, rotated_vectors, walkers):
    planes, walk = lax.axis_size("chol"), lax.axis_size("walk")
    depth = walk // 4
    chol, place = lax.axis_index("chol"), lax.axis_index("walk")
    core, z = place % 2, place // 4
    slab_vectors, slab_rows, orbitals = chol_vectors.shape
    occ = walkers.shape[2]
    swap = [(i, i ^ 1) for i in range(walk)]
    every = [(c, zz, y, k) for c in range(2) for zz in range(depth) for y in range(2) for k in range(2)]

    def send(array, target):
        pairs = [(flat(*at, walk), flat(*target(*at), walk)) for at in every if target(*at) is not None]
        return lax.ppermute(array, BOTH, pairs)

    other_vectors = lax.ppermute(rotated_vectors, "walk", swap)
    other_walker = lax.ppermute(walkers, "walk", swap)

    lanes = walkers.shape[2]
    spread = jnp.broadcast_to(field_draws.reshape(1, slab_vectors // lanes, lanes), (walk, slab_vectors // lanes, lanes))
    draws = lax.all_to_all(spread, "walk", split_axis=0, concat_axis=0, tiled=True)
    partial = partial_operators(draws, chol_vectors, planes)
    rows = lax.all_to_all(partial, BOTH, split_axis=0, concat_axis=0, tiled=True)
    other_rows = lax.ppermute(rows, "walk", swap)

    propagated, dual, own, other = solve(
        rows, other_rows, walkers[0], other_walker[0], rotated_vectors, other_vectors, planes
    )

    def first(c, zz, y, k):
        return (c, zz ^ 1 if zz // 2 == k else zz ^ 2, y, zz // 2)

    def second(c, zz, y, k):
        return (c, zz ^ 3, y, k) if zz // 2 == k else None

    turn = lambda c, zz, y, k: (c, zz, 1 - y, k) if k == 0 else (1 - c, zz, y, k)
    back = lambda c, zz, y, k: (1 - c, zz, y, k) if k == 0 else (c, zz, 1 - y, k)
    near, far = send(dual, first), send(dual, second)
    odd, inside = z % 2 == 1, z // 2 == core
    pick = lambda here, low, high: jnp.where(inside, jnp.where(here, dual, near), jnp.where(low, near, far))
    mine = jnp.stack([pick(~odd, ~odd, odd), pick(odd, odd, ~odd)])
    one, over = send(mine, turn), send(mine, back)
    terms = [energies(own, other, [mine])]
    one, propagated, terms[0] = lax.optimization_barrier((one, propagated, terms[0]))
    both = send(one, back)
    across = send(propagated, lambda c, zz, y, k: (1 - c, zz, y, k) if k == c else None)
    propagated = jnp.where(core == chol, propagated, across)[None]
    terms.append(energies(own, other, [one]))
    over, both, terms[1] = lax.optimization_barrier((over, both, terms[1]))
    terms.append(energies(own, other, [over, both]))
    terms = jnp.concatenate(terms, 0).sum(1)

    y = place // 2 % 2
    slots = []
    for order in range(4):
        first_axis, second_axis = order % 2, order // 2
        y_flip = jnp.where(core == 0, first_axis, second_axis)
        x_flip = jnp.where(core == 0, second_axis, first_axis)
        for parity in range(2):
            slots.append(((2 * core + parity) * 2 + (y ^ y_flip)) * 2 + (chol ^ x_flip))
    slots = jnp.stack(slots)
    hit = (slots[None, :, None] == jnp.arange(walk)[:, None, None]).astype(F32)
    sent = (hit * terms[None]).sum(1)
    sent = jnp.broadcast_to(sent, (planes,) + sent.shape).reshape(planes * walk, occ)
    came = lax.all_to_all(sent, BOTH, split_axis=0, concat_axis=0, tiled=True)
    return propagated, -0.5 * came.sum().reshape(1)


def per_device_plain(field_draws, chol_vectors, rotated_vectors, walkers):
    local_walkers, orbitals, occ = walkers.shape
    total_walkers = local_walkers * lax.axis_size("walk")
    slab_vectors, slab_rows, _ = chol_vectors.shape
    all_draws = lax.all_gather(field_draws, "walk", axis=0, tiled=True)
    partial_rows = jnp.dot(
        all_draws, chol_vectors.reshape(slab_vectors, slab_rows * orbitals), preferred_element_type=F32
    )
    partial_rows = partial_rows.reshape(total_walkers, slab_rows, orbitals)
    summed_rows = lax.psum(partial_rows, "chol").astype(BF)
    operators = lax.all_to_all(summed_rows, "walk", split_axis=0, concat_axis=1, tiled=True)
    propagated = jax.vmap(propagate)(operators, walkers)
    duals = jax.vmap(dual_of)(walkers, propagated)
    dual_cols = jnp.transpose(duals, (1, 0, 2)).reshape(orbitals, local_walkers * occ)
    columns = lax.all_gather(dual_cols, "walk", axis=1, tiled=True)

    def vector_step(vector, summed):
        single = lax.dynamic_index_in_dim(rotated_vectors, vector, 0, keepdims=False)
        tiled = jnp.dot(single, columns, preferred_element_type=F32).reshape(occ, total_walkers, occ)
        return summed + jnp.einsum("iwj,jwi->w", tiled, tiled)

    totals = lax.fori_loop(0, rotated_vectors.shape[0], vector_step, jnp.zeros((total_walkers,), F32))
    summed = lax.psum(totals, BOTH)
    mine = lax.dynamic_slice_in_dim(summed, lax.axis_index("walk") * local_walkers, local_walkers, 0)
    return propagated, -0.5 * mine


def solution(mesh):
    planes, walk = mesh.shape["chol"], mesh.shape["walk"]

    def step(field_draws, chol_vectors, rotated_vectors, walkers):
        rows, orbitals = chol_vectors.shape[1:]
        occ = walkers.shape[2]
        fits = planes == 2 and walk == 16 and walkers.shape[0] == 1 and rows == 2 * TILE and orbitals == GROUPS * occ
        body = per_device if fits else per_device_plain
        return body(field_draws, chol_vectors, rotated_vectors, walkers)

    return jax.shard_map(
        step,
        mesh=mesh,
        in_specs=(
            P("walk", "chol"),
            P("chol", "walk", None),
            P(("chol", "walk"), None, None),
            P("walk", None, None),
        ),
        out_specs=(P("walk", None, None), P("walk")),
        check_vma=False,
    )
```

time: 175 us -> 106 us (0.61)
  Pallas kernels: 67.4 us -> 38.4 us
  other arithmetic: 26.3 us -> 2.25 us
  blocking collectives: 13.5 us -> 32.2 us
  starting transfers between devices: 29.5 us -> 16 us
  waiting for transfers between devices: 26 us -> 13.2 us
  local copies, waits for them, and re-layouts: 4.89 us -> 0.7 us
  matrix products: 3.13 us -> 0 us
    pallas_call x4 -> x5, Pallas kernels: 67.4 us -> 38.4 us  [the longest x3 21.6 us: energies(): pl.pallas_call(functools.partial(energy_kernel, group, sub), in_specs=[vm...]
    another operation x7 -> x2, other arithmetic: 22.9 us -> 0.06 us  [per_device(): mine = jnp.stack([pick(~odd, ~odd, odd), pick(odd, odd, ~odd)])]
    all_to_all x1 -> x2, blocking collectives: 13.5 us -> 32.2 us  [the longest x1 18.7 us: per_device(): lax.all_to_all(partial, BOTH, split_axis=0, concat_axis=0, tiled=True)]
    all_to_all x1 -> x0, waiting for transfers between devices: 15.6 us -> none  [per_device(): lax.all_to_all(partial, BOTH, split_axis=0, concat_axis=0, tiled=True)]
    ppermute x10 -> x6, starting transfers between devices: 14.7 us -> 9.85 us  [send(): return lax.ppermute(array, BOTH, pairs)]
    all_to_all x1 -> x0, starting transfers between devices: 4.4 us -> none  [per_device(): lax.all_to_all(partial, BOTH, split_axis=0, concat_axis=0, tiled=True)]
    all_to_all x1, starting transfers between devices: 9.53 us -> 5.14 us  [per_device(): came = lax.all_to_all(sent, BOTH, split_axis=0, concat_axis=0, tiled=True)]
    unnamed x6 -> x2, local copies, waits for them, and re-layouts: 3.43 us -> 0.01 us
  transfers between devices with their start and end apart: 15 -> 10, of which waited for: 7 -> 6; matrix products, arithmetic and copies ran while one was open for 17% -> 2% of each run, Pallas kernels for 39% -> 30%
where the time goes in v2:
time: 106 us; the launch traced here: 105 us
  Pallas kernels  38.4 us (36%)
  blocking collectives  32.2 us (30%)
  starting transfers between devices  16 us (15%)
  waiting for transfers between devices  13.2 us (12%)
  between operations  2.53 us (2%)
  other arithmetic  2.25 us (2%)
    pallas_call x3, Pallas kernels, energies(): pl.pallas_call(functools.partial(energy_kernel, group, sub), in_specs=[vm...  21.6 us
    all_to_all x1, blocking collectives, per_device(): lax.all_to_all(partial, BOTH, split_axis=0, concat_axis=0, tiled=True)  18.7 us
    all_to_all x1, blocking collectives, per_device(): lax.all_to_all(spread, 'walk', split_axis=0, concat_axis=0, tiled=True)  13.5 us
    pallas_call x1, Pallas kernels, partial_operators(): pl.pallas_call(functools.partial(operator_kernel, planes), in_specs=[vmem...  10.2 us
    ppermute x6, starting transfers between devices, send(): return lax.ppermute(array, BOTH, pairs)  9.85 us
    pallas_call x1, Pallas kernels, solve(): pl.pallas_call(functools.partial(solve_kernel, planes), in_specs=[vmem] *...  6.68 us
    all_to_all x1, waiting for transfers between devices, per_device(): came = lax.all_to_all(sent, BOTH, split_axis=0, concat_axis=0, tiled=True)  6.4 us
    ppermute x6, waiting for transfers between devices, send(): return lax.ppermute(array, BOTH, pairs)  5.49 us
  transfers between devices with their start and end apart: 10, of which 6 were waited for; matrix products, arithmetic and copies ran while one was open for 2% of the time, Pallas kernels for 30%

profile of v2, /device:TPU:0, one launch (start us, length us, event | category | flops | bytes accessed | tf_op | source)
XLA Modules:
  0.0 105.3 jit_solution(1185653923038618544)
XLA Ops:
  0.6 0.5 collective-permute-start.2
  1.1 0.7 reduce.1
  1.9 13.5 %all_to_all.19.draws_ref = bf16[16,8,128]{2,1,0:T(8,128)(2,1)S(1)} all-to-all(bf16[16,8,128]{2,1,0:T(8,128)(2,1)S(1)} %broadcast_in_dim.17), channel_id=1, replica_groups=mesh['chol'=2,'walk'=16] {'walk'}, dimensions={0} | all-to-all | bytes 65536 | tf_op jit(solution)/shard_map/all_to_all | solution.py:338
  15.4 10.2 %operators.1 = bf16[32,16,384]{2,1,0:T(8,128)(2,1)S(1)} custom-call(bf16[16,8,128]{2,1,0:T(8,128)(2,1)S(1)} %all_to_all.19.draws_ref, bf16[1024,32,512]{2,1,0:T(8,128)(2,1)} %chol_ref.1), custom_call_target="tpu_custom_call" | custom-call | flops 5368709120 | bytes 20971520 | tf_op jit(solution)/shard_map/operators/pallas_call | solution.py:117
  25.5 18.7 %all_to_all.20.own_rows_ref = bf16[32,16,384]{2,1,0:T(8,128)(2,1)S(1)} all-to-all(bf16[32,16,384]{2,1,0:T(8,128)(2,1)S(1)} %operators.1), channel_id=1, replica_groups=mesh['chol'=2,'walk'=16] {'chol','walk'}, dimensions={0} | all-to-all | bytes 786432 | tf_op jit(solution)/shard_map/all_to_all | solution.py:340
  44.2 0.0 collective-permute-start
  44.2 0.5 collective-permute-start.1
  44.7 0.1 stack.47
  44.8 1.3 %collective-permute-done.1 = bf16[1,512,128]{2,1,0:T(8,128)(2,1)S(1)} collective-permute-done((bf16[1,512,128]{2,1,0:T(8,128)(2,1)S(1)}, bf16[1,512,128]{2,1,0:T(8,128)(2,1)S(1)}, u32[]{:S(2)}, u32[]{:S(2)}) %collective-permute-start.1) | collective-permute-done | bytes 131104 | tf_op jit(solution)/shard_map/ppermute | solution.py:334
  46.1 0.0 collective-permute-done.other_rows_ref
  46.1 0.0 collective-permute-done.2.other_ref
  46.1 6.7 %solve.1 = (f32[512,128]{1,0:T(8,128)S(1)}, bf16[512,128]{1,0:T(8,128)(2,1)S(1)}, bf16[64,128,512]{2,1,0:T(8,128)(2,1)S(1)}, bf16[64,128,512]{2,1,0:T(8,128)(2,1)S(1)}) custom-call(bf16[32,16,384]{2,1,0:T(8,128)(2,1)S(1)} %all_to_all.20.own_rows_ref, bf16[32,16,384]{2,1,0:T(8,128)(2,1)S(1)} %collective-permute-done.other_rows_ref, ...), custom_call_target="tpu_custom_call" | custom-call | flops 6000000000 | bytes 16777216 | tf_op jit(solution)/shard_map/solve/pallas_call | solution.py:249
  52.8 1.0 collective-permute-start.3
  53.8 4.2 %collective-permute-start.4 = (bf16[512,128]{1,0:T(8,128)(2,1)S(1)}, bf16[512,128]{1,0:T(8,128)(2,1)S(1)}, u32[]{:S(2)}, u32[]{:S(2)}) collective-permute-start(bf16[512,128]{1,0:T(8,128)(2,1)S(1)} %get-tuple-element.12), channel_id=1, source_target_pairs={{0,12},{2,14},{4,8},{6,10},{9,5},{11,7},{13,1},{15,3},{16,28},{18,... | collective-permute-start | bytes 393224 | tf_op jit(solution)/shard_map/ppermute | solution.py:331
  58.0 0.3 collective-permute-done.3
  58.3 2.0 %collective-permute-done.4 = bf16[512,128]{1,0:T(8,128)(2,1)S(1)} collective-permute-done((bf16[512,128]{1,0:T(8,128)(2,1)S(1)}, bf16[512,128]{1,0:T(8,128)(2,1)S(1)}, u32[]{:S(2)}, u32[]{:S(2)}) %collective-permute-start.4) | collective-permute-done | bytes 131104 | tf_op jit(solution)/shard_map/ppermute | solution.py:331
  60.4 0.6 collective-permute-start.5
  61.0 0.6 collective-permute-start.7
  61.5 5.7 %energies.3 = f32[2,8,128]{2,1,0:T(8,128)S(1)} custom-call(bf16[64,128,512]{2,1,0:T(8,128)(2,1)S(1)} %get-tuple-element.14.own_ref, bf16[64,128,512]{2,1,0:T(8,128)(2,1)S(1)} %get-tuple-element.15.other_ref, bf16[2,512,128]{2,1,0:T(8,128)(2,1)S(1)} %pad_maximum_fusion.refs_0_), custom_call_target="tpu_custom_call" | custom-call | flops 4294967296 | bytes 16777216 | tf_op jit(solution)/shard_map/energies/pallas_call | solution.py:300
  67.3 0.8 collective-permute-done.5.refs_0_
  68.1 3.4 %collective-permute-start.6 = (f32[512,128]{1,0:T(8,128)S(1)}, f32[512,128]{1,0:T(8,128)S(1)}, u32[]{:S(2)}, u32[]{:S(2)}) collective-permute-start(f32[512,128]{1,0:T(8,128)S(1)} %get-tuple-element.16), channel_id=1, source_target_pairs={{0,16},{2,18},{4,20},{6,22},{8,24},{10,26},{12,28},{14,30},{17,1},... | collective-permute-start | bytes 786440 | tf_op jit(solution)/shard_map/ppermute | solution.py:331
  71.6 0.1 collective-permute-start.8
  71.6 5.7 %energies.4 = f32[2,8,128]{2,1,0:T(8,128)S(1)} custom-call(bf16[64,128,512]{2,1,0:T(8,128)(2,1)S(1)} %get-tuple-element.14.own_ref, bf16[64,128,512]{2,1,0:T(8,128)(2,1)S(1)} %get-tuple-element.15.other_ref, bf16[2,512,128]{2,1,0:T(8,128)(2,1)S(1)} %collective-permute-done.5.refs_0_), custom_call_target="tpu_custom_call" | custom-call | flops 4294967296 | bytes 16777216 | tf_op jit(solution)/shard_map/energies/pallas_call | solution.py:300
  77.4 0.0 collective-permute-done.7.refs_0_
  77.4 2.4 %collective-permute-done.8.refs_1_ = bf16[2,512,128]{2,1,0:T(8,128)(2,1)S(1)} collective-permute-done((bf16[2,512,128]{2,1,0:T(8,128)(2,1)S(1)}, bf16[2,512,128]{2,1,0:T(8,128)(2,1)S(1)}, u32[]{:S(2)}, u32[]{:S(2)}) %collective-permute-start.8) | collective-permute-done | bytes 262176 | tf_op jit(solution)/shard_map/ppermute | solution.py:331
  79.8 10.1 %energies.5 = f32[4,8,128]{2,1,0:T(8,128)S(1)} custom-call(bf16[64,128,512]{2,1,0:T(8,128)(2,1)S(1)} %get-tuple-element.14.own_ref, bf16[64,128,512]{2,1,0:T(8,128)(2,1)S(1)} %get-tuple-element.15.other_ref, bf16[2,512,128]{2,1,0:T(8,128)(2,1)S(1)} %collective-permute-done.7.refs_0_, bf16[2,512,128]{2,1,0:T(8,128)(2,1)S(1)} %collective-permute-done.8.refs_1_), custom_call_target="tpu_custom_call" | custom-call | flops 8589934592 | bytes 16777216 | tf_op jit(solution)/shard_map/energies/pallas_call | solution.py:300
  89.9 0.1 multiply_reduce_fusion
  90.0 0.6 broadcast_in_dim.19
  90.6 5.1 %all-to-all-start.2 = ((f32[32,1,128]{2,1,0:T(1,128)}), f32[32,1,128]{2,1,0:T(1,128)S(1)}, u32[]{:S(2)}, u32[]{:S(2)}) async-start(f32[32,1,128]{2,1,0:T(1,128)} %bitcast.13), calls=%async_computation.2 | async-start | bytes 32768 | tf_op jit(solution)/shard_map/all_to_all | solution.py:382
  95.7 0.7 select_bitcast_fusion
  96.5 6.4 %all-to-all-done.2 = f32[32,1,128]{2,1,0:T(1,128)S(1)} async-done(((f32[32,1,128]{2,1,0:T(1,128)}), f32[32,1,128]{2,1,0:T(1,128)S(1)}, u32[]{:S(2)}, u32[]{:S(2)}) %all-to-all-start.2) | async-done | bytes 16416 | tf_op jit(solution)/shard_map/all_to_all | solution.py:382
  102.9 0.6 reduce_sum.29
  (8 shorter events, 0.1 us)
Async XLA Ops:
  0.6 45.5 %collective-permute-start.2 = (bf16[64,128,512]{2,1,0:T(8,128)(2,1)}, bf16[64,128,512]{2,1,0:T(8,128)(2,1)}, u32[]{:S(2)}, u32[]{:S(2)}) collective-permute-start(bf16[64,128,512]{2,1,0:T(8,128)(2,1)} %own_ref.1), channel_id=1, source_target_pairs={{0,1},{1,0},{2,3},{3,2},{4,5},{5,4},{6,7},{7,6},{8,9},{9,8},{10,11... | collective-permute-start | bytes 25165832 | tf_op jit(solution)/shard_map/ppermute | solution.py:333
  15.3 28.8 %copy-start = (bf16[1,512,128]{2,1,0:T(8,128)(2,1)S(1)}, bf16[1,512,128]{2,1,0:T(8,128)(2,1)}, u32[]{:S(2)}) copy-start(bf16[1,512,128]{2,1,0:T(8,128)(2,1)} %param.7) | copy-start | bytes 393220
  44.2 1.9 %collective-permute-start = (bf16[32,16,384]{2,1,0:T(8,128)(2,1)S(1)}, bf16[32,16,384]{2,1,0:T(8,128)(2,1)S(1)}, u32[]{:S(2)}, u32[]{:S(2)}) collective-permute-start(bf16[32,16,384]{2,1,0:T(8,128)(2,1)S(1)} %all_to_all.20.own_rows_ref), channel_id=1, source_target_pairs={{0,1},{1,0},{2,3},{3,2},{4,5},{5,4},{6,7},{7,6},{8,9},{9,8},{10,11... | collective-permute-start | bytes 1179656 | tf_op jit(solution)/shard_map/ppermute | solution.py:341
  44.2 1.9 %collective-permute-start.1 = (bf16[1,512,128]{2,1,0:T(8,128)(2,1)S(1)}, bf16[1,512,128]{2,1,0:T(8,128)(2,1)S(1)}, u32[]{:S(2)}, u32[]{:S(2)}) collective-permute-start(bf16[1,512,128]{2,1,0:T(8,128)(2,1)S(1)} %copy-done), channel_id=1, source_target_pairs={{0,1},{1,0},{2,3},{3,2},{4,5},{5,4},{6,7},{7,6},{8,9},{9,8},{10,11... | collective-permute-start | bytes 393224 | tf_op jit(solution)/shard_map/ppermute | solution.py:334
  52.8 5.5 %collective-permute-start.3 = (bf16[512,128]{1,0:T(8,128)(2,1)S(1)}, bf16[512,128]{1,0:T(8,128)(2,1)S(1)}, u32[]{:S(2)}, u32[]{:S(2)}) collective-permute-start(bf16[512,128]{1,0:T(8,128)(2,1)S(1)} %get-tuple-element.12), channel_id=1, source_target_pairs={{0,4},{1,8},{2,6},{3,10},{4,0},{5,12},{6,2},{7,14},{8,1},{9,13},{1... | collective-permute-start | bytes 393224 | tf_op jit(solution)/shard_map/ppermute | solution.py:331
  53.8 6.5 %collective-permute-start.4 = (bf16[512,128]{1,0:T(8,128)(2,1)S(1)}, bf16[512,128]{1,0:T(8,128)(2,1)S(1)}, u32[]{:S(2)}, u32[]{:S(2)}) collective-permute-start(bf16[512,128]{1,0:T(8,128)(2,1)S(1)} %get-tuple-element.12), channel_id=1, source_target_pairs={{0,12},{2,14},{4,8},{6,10},{9,5},{11,7},{13,1},{15,3},{16,28},{18,... | collective-permute-start | bytes 393224 | tf_op jit(solution)/shard_map/ppermute | solution.py:331
  60.4 7.7 %collective-permute-start.5 = (bf16[2,512,128]{2,1,0:T(8,128)(2,1)S(1)}, bf16[2,512,128]{2,1,0:T(8,128)(2,1)S(1)}, u32[]{:S(2)}, u32[]{:S(2)}) collective-permute-start(bf16[2,512,128]{2,1,0:T(8,128)(2,1)S(1)} %pad_maximum_fusion.refs_0_), channel_id=1, source_target_pairs={{0,2},{1,17},{2,0},{3,19},{4,6},{5,21},{6,4},{7,23},{8,10},{9,25},... | collective-permute-start | bytes 786440 | tf_op jit(solution)/shard_map/ppermute | solution.py:331
  61.0 16.4 %collective-permute-start.7 = (bf16[2,512,128]{2,1,0:T(8,128)(2,1)S(1)}, bf16[2,512,128]{2,1,0:T(8,128)(2,1)S(1)}, u32[]{:S(2)}, u32[]{:S(2)}) collective-permute-start(bf16[2,512,128]{2,1,0:T(8,128)(2,1)S(1)} %pad_maximum_fusion.refs_0_), channel_id=1, source_target_pairs={{0,16},{1,3},{2,18},{3,1},{4,20},{5,7},{6,22},{7,5},{8,24},{9,11},... | collective-permute-start | bytes 786440 | tf_op jit(solution)/shard_map/ppermute | solution.py:331
  68.1 27.6 %collective-permute-start.6 = (f32[512,128]{1,0:T(8,128)S(1)}, f32[512,128]{1,0:T(8,128)S(1)}, u32[]{:S(2)}, u32[]{:S(2)}) collective-permute-start(f32[512,128]{1,0:T(8,128)S(1)} %get-tuple-element.16), channel_id=1, source_target_pairs={{0,16},{2,18},{4,20},{6,22},{8,24},{10,26},{12,28},{14,30},{17,1},... | collective-permute-start | bytes 786440 | tf_op jit(solution)/shard_map/ppermute | solution.py:331
  71.6 8.2 %collective-permute-start.8 = (bf16[2,512,128]{2,1,0:T(8,128)(2,1)S(1)}, bf16[2,512,128]{2,1,0:T(8,128)(2,1)S(1)}, u32[]{:S(2)}, u32[]{:S(2)}) collective-permute-start(bf16[2,512,128]{2,1,0:T(8,128)(2,1)S(1)} %collective-permute-done.5.refs_0_), channel_id=1, source_target_pairs={{0,16},{1,3},{2,18},{3,1},{4,20},{5,7},{6,22},{7,5},{8,24},{9,11},... | collective-permute-start | bytes 786440 | tf_op jit(solution)/shard_map/ppermute | solution.py:331
  90.6 12.3 %all-to-all-start.2 = ((f32[32,1,128]{2,1,0:T(1,128)}), f32[32,1,128]{2,1,0:T(1,128)S(1)}, u32[]{:S(2)}, u32[]{:S(2)}) async-start(f32[32,1,128]{2,1,0:T(1,128)} %bitcast.13), calls=%async_computation.2 | async-start | bytes 32768 | tf_op jit(solution)/shard_map/all_to_all | solution.py:382

commit v3 on v2

--- a/solution.py
+++ b/solution.py
@@ -293,7 +293,7 @@
                 out_ref[slot] += totals[slot]
 
 
-def energies(own, other, duals, group=32, sub=2):
+def energies(own, other, duals, group=64, sub=2):
     vectors, occ, orbitals = own.shape
     count = 2 * len(duals)
     vmem = pl.BlockSpec(memory_space=pltpu.VMEM)
@@ -356,15 +356,17 @@
     odd, inside = z % 2 == 1, z // 2 == core
     pick = lambda here, low, high: jnp.where(inside, jnp.where(here, dual, near), jnp.where(low, near, far))
     mine = jnp.stack([pick(~odd, ~odd, odd), pick(odd, odd, ~odd)])
-    one, over = send(mine, turn), send(mine, back)
+    across = send(propagated, lambda c, zz, y, k: (1 - c, zz, y, k) if k == c else None)
+    one = send(mine, turn)
     terms = [energies(own, other, [mine])]
-    one, propagated, terms[0] = lax.optimization_barrier((one, propagated, terms[0]))
+    one, mine, terms[0] = lax.optimization_barrier((one, mine, terms[0]))
+    over = send(mine, back)
+    terms.append(energies(own, other, [one]))
+    one, over, terms[1] = lax.optimization_barrier((one, over, terms[1]))
     both = send(one, back)
-    across = send(propagated, lambda c, zz, y, k: (1 - c, zz, y, k) if k == c else None)
-    propagated = jnp.where(core == chol, propagated, across)[None]
-    terms.append(energies(own, other, [one]))
-    over, both, terms[1] = lax.optimization_barrier((over, both, terms[1]))
-    terms.append(energies(own, other, [over, both]))
+    terms.append(energies(own, other, [over]))
+    both, terms[2] = lax.optimization_barrier((both, terms[2]))
+    terms.append(energies(own, other, [both]))
     terms = jnp.concatenate(terms, 0).sum(1)
 
     y = place // 2 % 2
@@ -380,6 +382,7 @@
     sent = (hit * terms[None]).sum(1)
     sent = jnp.broadcast_to(sent, (planes,) + sent.shape).reshape(planes * walk, occ)
     came = lax.all_to_all(sent, BOTH, split_axis=0, concat_axis=0, tiled=True)
+    propagated = jnp.where(core == chol, propagated, across)[None]
     return propagated, -0.5 * came.sum().reshape(1)
 
 

time: 106 us -> 101 us (0.953)
  waiting for transfers between devices: 13.2 us -> 11.1 us
  Pallas kernels: 38.4 us -> 36.4 us
    ppermute x6, waiting for transfers between devices: 5.49 us -> 3.41 us  [send(): return lax.ppermute(array, BOTH, pairs)]
    pallas_call x3 -> x4, Pallas kernels: 21.6 us -> 19.5 us  [energies(): pl.pallas_call(functools.partial(energy_kernel, group, sub), in_specs=[vm...]
  transfers between devices with their start and end apart: 10 -> 10, of which waited for: 6 -> 5; matrix products, arithmetic and copies ran while one was open for 2% -> 2% of each run, Pallas kernels for 30% -> 30%
where the time goes in v3:
time: 101 us; the launch traced here: 100 us
  Pallas kernels  36.4 us (36%)
  blocking collectives  32.2 us (32%)
  starting transfers between devices  15.1 us (15%)
  waiting for transfers between devices  11.1 us (11%)
  between operations  2.53 us (3%)
  other arithmetic  2.26 us (2%)
    pallas_call x4, Pallas kernels, energies(): pl.pallas_call(functools.partial(energy_kernel, group, sub), in_specs=[vm...  19.5 us
    all_to_all x1, blocking collectives, per_device(): lax.all_to_all(partial, BOTH, split_axis=0, concat_axis=0, tiled=True)  18.7 us
    all_to_all x1, blocking collectives, per_device(): lax.all_to_all(spread, 'walk', split_axis=0, concat_axis=0, tiled=True)  13.5 us
    pallas_call x1, Pallas kernels, partial_operators(): pl.pallas_call(functools.partial(operator_kernel, planes), in_specs=[vmem...  10.2 us
    ppermute x6, starting transfers between devices, send(): return lax.ppermute(array, BOTH, pairs)  9.16 us
    pallas_call x1, Pallas kernels, solve(): pl.pallas_call(functools.partial(solve_kernel, planes), in_specs=[vmem] *...  6.68 us
    all_to_all x1, waiting for transfers between devices, per_device(): came = lax.all_to_all(sent, BOTH, split_axis=0, concat_axis=0, tiled=True)  6.4 us
    all_to_all x1, starting transfers between devices, per_device(): came = lax.all_to_all(sent, BOTH, split_axis=0, concat_axis=0, tiled=True)  4.9 us
  transfers between devices with their start and end apart: 10, of which 5 were waited for; matrix products, arithmetic and copies ran while one was open for 2% of the time, Pallas kernels for 30%

profile of v3, /device:TPU:0, one launch (start us, length us, event | category | flops | bytes accessed | tf_op | source)
XLA Modules:
  0.0 100.2 jit_solution(5398714138591920678)
XLA Ops:
  0.6 0.5 collective-permute-start.2
  1.1 0.7 reduce.1
  1.9 13.5 %all_to_all.19.draws_ref = bf16[16,8,128]{2,1,0:T(8,128)(2,1)S(1)} all-to-all(bf16[16,8,128]{2,1,0:T(8,128)(2,1)S(1)} %broadcast_in_dim.17), channel_id=1, replica_groups=mesh['chol'=2,'walk'=16] {'walk'}, dimensions={0} | all-to-all | bytes 65536 | tf_op jit(solution)/shard_map/all_to_all | solution.py:338
  15.4 10.2 %operators.1 = bf16[32,16,384]{2,1,0:T(8,128)(2,1)S(1)} custom-call(bf16[16,8,128]{2,1,0:T(8,128)(2,1)S(1)} %all_to_all.19.draws_ref, bf16[1024,32,512]{2,1,0:T(8,128)(2,1)} %chol_ref.1), custom_call_target="tpu_custom_call" | custom-call | flops 5368709120 | bytes 20971520 | tf_op jit(solution)/shard_map/operators/pallas_call | solution.py:117
  25.5 18.7 %all_to_all.20.own_rows_ref = bf16[32,16,384]{2,1,0:T(8,128)(2,1)S(1)} all-to-all(bf16[32,16,384]{2,1,0:T(8,128)(2,1)S(1)} %operators.1), channel_id=1, replica_groups=mesh['chol'=2,'walk'=16] {'chol','walk'}, dimensions={0} | all-to-all | bytes 786432 | tf_op jit(solution)/shard_map/all_to_all | solution.py:340
  44.2 0.0 collective-permute-start
  44.2 0.5 collective-permute-start.1
  44.7 0.1 stack.44
  44.8 1.3 %collective-permute-done.1 = bf16[1,512,128]{2,1,0:T(8,128)(2,1)S(1)} collective-permute-done((bf16[1,512,128]{2,1,0:T(8,128)(2,1)S(1)}, bf16[1,512,128]{2,1,0:T(8,128)(2,1)S(1)}, u32[]{:S(2)}, u32[]{:S(2)}) %collective-permute-start.1) | collective-permute-done | bytes 131104 | tf_op jit(solution)/shard_map/ppermute | solution.py:334
  46.1 0.0 collective-permute-done.other_rows_ref
  46.1 6.7 %solve.1 = (f32[512,128]{1,0:T(8,128)S(1)}, bf16[512,128]{1,0:T(8,128)(2,1)S(1)}, bf16[64,128,512]{2,1,0:T(8,128)(2,1)S(1)}, bf16[64,128,512]{2,1,0:T(8,128)(2,1)S(1)}) custom-call(bf16[32,16,384]{2,1,0:T(8,128)(2,1)S(1)} %all_to_all.20.own_rows_ref, bf16[32,16,384]{2,1,0:T(8,128)(2,1)S(1)} %collective-permute-done.other_rows_ref, ...), custom_call_target="tpu_custom_call" | custom-call | flops 6000000000 | bytes 16777216 | tf_op jit(solution)/shard_map/solve/pallas_call | solution.py:249
  52.8 1.0 collective-permute-start.4
  53.8 4.0 %collective-permute-start.5 = (bf16[512,128]{1,0:T(8,128)(2,1)S(1)}, bf16[512,128]{1,0:T(8,128)(2,1)S(1)}, u32[]{:S(2)}, u32[]{:S(2)}) collective-permute-start(bf16[512,128]{1,0:T(8,128)(2,1)S(1)} %get-tuple-element.15), channel_id=1, source_target_pairs={{0,12},{2,14},{4,8},{6,10},{9,5},{11,7},{13,1},{15,3},{16,28},{18,... | collective-permute-start | bytes 393224 | tf_op jit(solution)/shard_map/ppermute | solution.py:331
  57.8 3.1 %collective-permute-start.3 = (f32[512,128]{1,0:T(8,128)S(1)}, f32[512,128]{1,0:T(8,128)S(1)}, u32[]{:S(2)}, u32[]{:S(2)}) collective-permute-start(f32[512,128]{1,0:T(8,128)S(1)} %get-tuple-element.14), channel_id=1, source_target_pairs={{0,16},{2,18},{4,20},{6,22},{8,24},{10,26},{12,28},{14,30},{17,1},... | collective-permute-start | bytes 786440 | tf_op jit(solution)/shard_map/ppermute | solution.py:331
  60.9 0.0 collective-permute-done.5
  61.0 0.2 collective-permute-start.6
  61.2 4.8 %energies.4 = f32[2,8,128]{2,1,0:T(8,128)S(1)} custom-call(bf16[64,128,512]{2,1,0:T(8,128)(2,1)S(1)} %get-tuple-element.16.own_ref, bf16[64,128,512]{2,1,0:T(8,128)(2,1)S(1)} %get-tuple-element.17.other_ref, bf16[2,512,128]{2,1,0:T(8,128)(2,1)S(1)} %pad_maximum_fusion.refs_0_), custom_call_target="tpu_custom_call" | custom-call | flops 4294967296 | bytes 16777216 | tf_op jit(solution)/shard_map/energies/pallas_call | solution.py:300
  66.0 1.5 %collective-permute-done.6.refs_0_ = bf16[2,512,128]{2,1,0:T(8,128)(2,1)S(1)} collective-permute-done((bf16[2,512,128]{2,1,0:T(8,128)(2,1)S(1)}, bf16[2,512,128]{2,1,0:T(8,128)(2,1)S(1)}, u32[]{:S(2)}, u32[]{:S(2)}) %collective-permute-start.6) | collective-permute-done | bytes 262176 | tf_op jit(solution)/shard_map/ppermute | solution.py:331
  67.5 0.4 collective-permute-start.7
  67.8 4.8 %energies.5 = f32[2,8,128]{2,1,0:T(8,128)S(1)} custom-call(bf16[64,128,512]{2,1,0:T(8,128)(2,1)S(1)} %get-tuple-element.16.own_ref, bf16[64,128,512]{2,1,0:T(8,128)(2,1)S(1)} %get-tuple-element.17.other_ref, bf16[2,512,128]{2,1,0:T(8,128)(2,1)S(1)} %collective-permute-done.6.refs_0_), custom_call_target="tpu_custom_call" | custom-call | flops 4294967296 | bytes 16777216 | tf_op jit(solution)/shard_map/energies/pallas_call | solution.py:300
  72.6 1.2 %collective-permute-done.7.refs_0_ = bf16[2,512,128]{2,1,0:T(8,128)(2,1)S(1)} collective-permute-done((bf16[2,512,128]{2,1,0:T(8,128)(2,1)S(1)}, bf16[2,512,128]{2,1,0:T(8,128)(2,1)S(1)}, u32[]{:S(2)}, u32[]{:S(2)}) %collective-permute-start.7) | collective-permute-done | bytes 262176 | tf_op jit(solution)/shard_map/ppermute | solution.py:331
  73.8 0.6 collective-permute-start.8
  74.4 5.1 %energies.6 = f32[2,8,128]{2,1,0:T(8,128)S(1)} custom-call(bf16[64,128,512]{2,1,0:T(8,128)(2,1)S(1)} %get-tuple-element.16.own_ref, bf16[64,128,512]{2,1,0:T(8,128)(2,1)S(1)} %get-tuple-element.17.other_ref, bf16[2,512,128]{2,1,0:T(8,128)(2,1)S(1)} %collective-permute-done.7.refs_0_), custom_call_target="tpu_custom_call" | custom-call | flops 4294967296 | bytes 16777216 | tf_op jit(solution)/shard_map/energies/pallas_call | solution.py:300
  79.4 0.8 collective-permute-done.8.refs_0_
  80.2 4.8 %energies.7 = f32[2,8,128]{2,1,0:T(8,128)S(1)} custom-call(bf16[64,128,512]{2,1,0:T(8,128)(2,1)S(1)} %get-tuple-element.16.own_ref, bf16[64,128,512]{2,1,0:T(8,128)(2,1)S(1)} %get-tuple-element.17.other_ref, bf16[2,512,128]{2,1,0:T(8,128)(2,1)S(1)} %collective-permute-done.8.refs_0_), custom_call_target="tpu_custom_call" | custom-call | flops 4294967296 | bytes 16777216 | tf_op jit(solution)/shard_map/energies/pallas_call | solution.py:300
  85.0 0.1 multiply_reduce_fusion
  85.1 0.6 broadcast_in_dim.19
  85.7 4.9 %all-to-all-start.2 = ((f32[32,1,128]{2,1,0:T(1,128)}), f32[32,1,128]{2,1,0:T(1,128)S(1)}, u32[]{:S(2)}, u32[]{:S(2)}) async-start(f32[32,1,128]{2,1,0:T(1,128)} %bitcast.13), calls=%async_computation.2 | async-start | bytes 32768 | tf_op jit(solution)/shard_map/all_to_all | solution.py:384
  90.7 0.0 collective-permute-done.3
  90.7 0.7 select_bitcast_fusion
  91.4 6.4 %all-to-all-done.2 = f32[32,1,128]{2,1,0:T(1,128)S(1)} async-done(((f32[32,1,128]{2,1,0:T(1,128)}), f32[32,1,128]{2,1,0:T(1,128)S(1)}, u32[]{:S(2)}, u32[]{:S(2)}) %all-to-all-start.2) | async-done | bytes 16416 | tf_op jit(solution)/shard_map/all_to_all | solution.py:384
  97.8 0.6 reduce_sum.29
  (9 shorter events, 0.1 us)
Async XLA Ops:
  0.6 45.5 %collective-permute-start.2 = (bf16[64,128,512]{2,1,0:T(8,128)(2,1)}, bf16[64,128,512]{2,1,0:T(8,128)(2,1)}, u32[]{:S(2)}, u32[]{:S(2)}) collective-permute-start(bf16[64,128,512]{2,1,0:T(8,128)(2,1)} %own_ref.1), channel_id=1, source_target_pairs={{0,1},{1,0},{2,3},{3,2},{4,5},{5,4},{6,7},{7,6},{8,9},{9,8},{10,11... | collective-permute-start | bytes 25165832 | tf_op jit(solution)/shard_map/ppermute | solution.py:333
  15.3 28.8 %copy-start = (bf16[1,512,128]{2,1,0:T(8,128)(2,1)S(1)}, bf16[1,512,128]{2,1,0:T(8,128)(2,1)}, u32[]{:S(2)}) copy-start(bf16[1,512,128]{2,1,0:T(8,128)(2,1)} %param.7) | copy-start | bytes 393220
  44.2 1.9 %collective-permute-start = (bf16[32,16,384]{2,1,0:T(8,128)(2,1)S(1)}, bf16[32,16,384]{2,1,0:T(8,128)(2,1)S(1)}, u32[]{:S(2)}, u32[]{:S(2)}) collective-permute-start(bf16[32,16,384]{2,1,0:T(8,128)(2,1)S(1)} %all_to_all.20.own_rows_ref), channel_id=1, source_target_pairs={{0,1},{1,0},{2,3},{3,2},{4,5},{5,4},{6,7},{7,6},{8,9},{9,8},{10,11... | collective-permute-start | bytes 1179656 | tf_op jit(solution)/shard_map/ppermute | solution.py:341
  44.2 1.9 %collective-permute-start.1 = (bf16[1,512,128]{2,1,0:T(8,128)(2,1)S(1)}, bf16[1,512,128]{2,1,0:T(8,128)(2,1)S(1)}, u32[]{:S(2)}, u32[]{:S(2)}) collective-permute-start(bf16[1,512,128]{2,1,0:T(8,128)(2,1)S(1)} %copy-done), channel_id=1, source_target_pairs={{0,1},{1,0},{2,3},{3,2},{4,5},{5,4},{6,7},{7,6},{8,9},{9,8},{10,11... | collective-permute-start | bytes 393224 | tf_op jit(solution)/shard_map/ppermute | solution.py:334
  52.8 8.1 %collective-permute-start.4 = (bf16[512,128]{1,0:T(8,128)(2,1)S(1)}, bf16[512,128]{1,0:T(8,128)(2,1)S(1)}, u32[]{:S(2)}, u32[]{:S(2)}) collective-permute-start(bf16[512,128]{1,0:T(8,128)(2,1)S(1)} %get-tuple-element.15), channel_id=1, source_target_pairs={{0,4},{1,8},{2,6},{3,10},{4,0},{5,12},{6,2},{7,14},{8,1},{9,13},{1... | collective-permute-start | bytes 393224 | tf_op jit(solution)/shard_map/ppermute | solution.py:331
  53.8 7.2 %collective-permute-start.5 = (bf16[512,128]{1,0:T(8,128)(2,1)S(1)}, bf16[512,128]{1,0:T(8,128)(2,1)S(1)}, u32[]{:S(2)}, u32[]{:S(2)}) collective-permute-start(bf16[512,128]{1,0:T(8,128)(2,1)S(1)} %get-tuple-element.15), channel_id=1, source_target_pairs={{0,12},{2,14},{4,8},{6,10},{9,5},{11,7},{13,1},{15,3},{16,28},{18,... | collective-permute-start | bytes 393224 | tf_op jit(solution)/shard_map/ppermute | solution.py:331
  57.8 32.9 %collective-permute-start.3 = (f32[512,128]{1,0:T(8,128)S(1)}, f32[512,128]{1,0:T(8,128)S(1)}, u32[]{:S(2)}, u32[]{:S(2)}) collective-permute-start(f32[512,128]{1,0:T(8,128)S(1)} %get-tuple-element.14), channel_id=1, source_target_pairs={{0,16},{2,18},{4,20},{6,22},{8,24},{10,26},{12,28},{14,30},{17,1},... | collective-permute-start | bytes 786440 | tf_op jit(solution)/shard_map/ppermute | solution.py:331
  61.0 6.4 %collective-permute-start.6 = (bf16[2,512,128]{2,1,0:T(8,128)(2,1)S(1)}, bf16[2,512,128]{2,1,0:T(8,128)(2,1)S(1)}, u32[]{:S(2)}, u32[]{:S(2)}) collective-permute-start(bf16[2,512,128]{2,1,0:T(8,128)(2,1)S(1)} %pad_maximum_fusion.refs_0_), channel_id=1, source_target_pairs={{0,2},{1,17},{2,0},{3,19},{4,6},{5,21},{6,4},{7,23},{8,10},{9,25},... | collective-permute-start | bytes 786440 | tf_op jit(solution)/shard_map/ppermute | solution.py:331
  67.5 6.4 %collective-permute-start.7 = (bf16[2,512,128]{2,1,0:T(8,128)(2,1)S(1)}, bf16[2,512,128]{2,1,0:T(8,128)(2,1)S(1)}, u32[]{:S(2)}, u32[]{:S(2)}) collective-permute-start(bf16[2,512,128]{2,1,0:T(8,128)(2,1)S(1)} %pad_maximum_fusion.refs_0_), channel_id=1, source_target_pairs={{0,16},{1,3},{2,18},{3,1},{4,20},{5,7},{6,22},{7,5},{8,24},{9,11},... | collective-permute-start | bytes 786440 | tf_op jit(solution)/shard_map/ppermute | solution.py:331
  73.8 6.4 %collective-permute-start.8 = (bf16[2,512,128]{2,1,0:T(8,128)(2,1)S(1)}, bf16[2,512,128]{2,1,0:T(8,128)(2,1)S(1)}, u32[]{:S(2)}, u32[]{:S(2)}) collective-permute-start(bf16[2,512,128]{2,1,0:T(8,128)(2,1)S(1)} %collective-permute-done.6.refs_0_), channel_id=1, source_target_pairs={{0,16},{1,3},{2,18},{3,1},{4,20},{5,7},{6,22},{7,5},{8,24},{9,11},... | collective-permute-start | bytes 786440 | tf_op jit(solution)/shard_map/ppermute | solution.py:331
  85.7 12.1 %all-to-all-start.2 = ((f32[32,1,128]{2,1,0:T(1,128)}), f32[32,1,128]{2,1,0:T(1,128)S(1)}, u32[]{:S(2)}, u32[]{:S(2)}) async-start(f32[32,1,128]{2,1,0:T(1,128)} %bitcast.13), calls=%async_computation.2 | async-start | bytes 32768 | tf_op jit(solution)/shard_map/all_to_all | solution.py:384

commit v4 on v3

--- a/solution.py
+++ b/solution.py
@@ -10,6 +10,7 @@
 TERMS = 4
 TILE = 16
 GROUPS = 4
+PRELOADED = 1
 BF = jnp.bfloat16
 F32 = jnp.float32
 BOTH = ("chol", "walk")
@@ -45,28 +46,70 @@
     return solve_dual(correlation, propagated.T).T.astype(BF)
 
 
-def operator_kernel(planes, draws_ref, chol_ref, out_ref, near_ref, far_ref, repeat_ref, spread_ref, sums_ref, sems):
+def column_copies(chol_ref, near_refs, far_refs, sems, first, group):
+    rows, orbitals = chol_ref.shape[1:]
+    wide = orbitals // GROUPS
+    own_group = lax.axis_index("walk") * rows // wide
+    upper = jnp.where(own_group >= GROUPS // 2, 1, 0)
+
+    def columns(shift):
+        return pl.ds(pl.multiple_of((own_group + shift) % GROUPS * wide, wide), wide)
+
+    copies = []
+    for at, (near_ref, far_ref) in enumerate(zip(near_refs, far_refs)):
+        start = (first + at) * group
+        whole, half = pl.ds(start, group), pl.ds(start + upper * (group // 2), group // 2)
+        pairs = [
+            (chol_ref.at[whole, :, columns(0)], near_ref.at[:, :, pl.ds(0, wide)]),
+            (chol_ref.at[whole, :, columns(1)], near_ref.at[:, :, pl.ds(wide, wide)]),
+            (chol_ref.at[half, :, columns(2)], far_ref),
+        ]
+        copies.append([pltpu.make_async_copy(*pair, sems.at[at, nth]) for nth, pair in enumerate(pairs)])
+    return copies, upper
+
+
+def preload_kernel(group, chol_ref, *refs):
+    steps = len(refs) // 2
+    copies, _ = column_copies(chol_ref, refs[:steps], refs[steps:-1], refs[-1], 0, group)
+    for step in copies:
+        for copy in step:
+            copy.start()
+    for step in copies:
+        for copy in step:
+            copy.wait()
+
+
+def preload(chol_vectors, steps, group):
+    _, rows, orbitals = chol_vectors.shape
+    wide = orbitals // GROUPS
+    return pl.pallas_call(
+        functools.partial(preload_kernel, group),
+        in_specs=[pl.BlockSpec(memory_space=pl.ANY)],
+        out_specs=[pl.BlockSpec(memory_space=pltpu.VMEM)] * (2 * steps),
+        out_shape=[pltpu.VMEM((group, rows, 2 * wide), BF)] * steps
+        + [pltpu.VMEM((group // 2, rows, wide), BF)] * steps,
+        scratch_shapes=[pltpu.SemaphoreType.DMA((steps, 3))],
+        compiler_params=pltpu.CompilerParams(vmem_limit_bytes=1 << 20),
+        cost_estimate=pl.CostEstimate(
+            flops=0, bytes_accessed=10 * steps * group * rows * wide, transcendentals=0
+        ),
+        name="preload",
+    )(in_hbm(chol_vectors))
+
+
+def operator_kernel(planes, loaded, draws_ref, *refs):
+    near_refs, far_refs = list(refs[:loaded]), list(refs[loaded : 2 * loaded])
+    chol_ref, out_ref, near_ref, far_ref, repeat_ref, spread_ref, sums_ref, sems = refs[2 * loaded :]
     walkers, steps, group = draws_ref.shape
     rows, orbitals = chol_ref.shape[1:]
     wide = orbitals // GROUPS
     depth = group * TILE
     parts = rows // TILE
-    own_group = lax.axis_index("walk") * rows // wide
-    upper = jnp.where(own_group >= GROUPS // 2, 1, 0)
-
-    def columns(shift):
-        return pl.ds(pl.multiple_of((own_group + shift) % GROUPS * wide, wide), wide)
-
-    copies = []
-    for step in range(steps):
-        whole, half = pl.ds(step * group, group), pl.ds(step * group + upper * (group // 2), group // 2)
-        pairs = [
-            (chol_ref.at[whole, :, columns(0)], near_ref.at[step, :, :, pl.ds(0, wide)]),
-            (chol_ref.at[whole, :, columns(1)], near_ref.at[step, :, :, pl.ds(wide, wide)]),
-            (chol_ref.at[half, :, columns(2)], far_ref.at[step]),
-        ]
-        copies.append([pltpu.make_async_copy(*pair, sems.at[step, at]) for at, pair in enumerate(pairs)])
-        for copy in copies[-1]:
+    rest = [near_ref.at[at] for at in range(steps - loaded)], [far_ref.at[at] for at in range(steps - loaded)]
+    near_refs, far_refs = near_refs + rest[0], far_refs + rest[1]
+    copies, upper = column_copies(chol_ref, *rest, sems, loaded, group)
+    for step in copies:
+        for copy in step:
             copy.start()
 
     owner = lax.broadcasted_iota(jnp.int32, (group, depth), 1) // TILE
@@ -90,14 +133,16 @@
     for step in range(steps):
         if step + 1 < steps:
             spread(step + 1)
-        for copy in copies[step]:
-            copy.wait()
+        near, far_at = near_refs[step], far_refs[step]
+        if step >= loaded:
+            for copy in copies[step - loaded]:
+                copy.wait()
         far = []
         for part in range(parts):
             taken = slice(part * TILE, (part + 1) * TILE)
-            right = near_ref[step, :, taken, :].reshape(depth, 2 * wide)
+            right = near[:, taken, :].reshape(depth, 2 * wide)
             add(part, step, jnp.dot(spread_ref[step % 2], right, preferred_element_type=F32))
-            far.append(far_ref[step, :, taken, :].reshape(depth // 2, wide))
+            far.append(far_at[:, taken, :].reshape(depth // 2, wide))
         right = jnp.concatenate(far, axis=1)
         add(parts, step, jnp.dot(spread_ref[step % 2, :, half_lanes], right, preferred_element_type=F32))
 
@@ -109,32 +154,34 @@
             out_ref[place, :, 2 * wide :] = sums_ref[parts, taken, part * wide : (part + 1) * wide].astype(BF)
 
 
-def partial_operators(draws, chol_vectors, planes):
+def partial_operators(draws, chol_vectors, held, planes):
     walkers, steps, group = draws.shape
     vectors, rows, orbitals = chol_vectors.shape
     parts, wide = rows // TILE, orbitals // GROUPS
+    loaded = len(held) // 2
+    rest = steps - loaded
     vmem = pl.BlockSpec(memory_space=pltpu.VMEM)
     return pl.pallas_call(
-        functools.partial(operator_kernel, planes),
-        in_specs=[vmem, pl.BlockSpec(memory_space=pl.ANY)],
+        functools.partial(operator_kernel, planes, loaded),
+        in_specs=[vmem] * (1 + len(held)) + [pl.BlockSpec(memory_space=pl.ANY)],
         out_specs=vmem,
         out_shape=jax.ShapeDtypeStruct((walkers * parts, TILE, 3 * wide), BF),
         scratch_shapes=[
-            pltpu.VMEM((steps, group, rows, 2 * wide), BF),
-            pltpu.VMEM((steps, group // 2, rows, wide), BF),
+            pltpu.VMEM((rest, group, rows, 2 * wide), BF),
+            pltpu.VMEM((rest, group // 2, rows, wide), BF),
             pltpu.VMEM((group, group * TILE), BF),
             pltpu.VMEM((2, walkers * TILE, group * TILE), BF),
             pltpu.VMEM((parts + 1, walkers * TILE, 2 * wide), F32),
-            pltpu.SemaphoreType.DMA((steps, 3)),
+            pltpu.SemaphoreType.DMA((rest, 3)),
         ],
-        compiler_params=pltpu.CompilerParams(vmem_limit_bytes=32 << 20),
+        compiler_params=pltpu.CompilerParams(vmem_limit_bytes=24 << 20),
         cost_estimate=pl.CostEstimate(
             flops=10 * walkers * TILE * vectors * rows * wide // 2,
             bytes_accessed=vectors * rows * wide * 5,
             transcendentals=0,
         ),
         name="operators",
-    )(draws, in_hbm(chol_vectors))
+    )(draws, *[in_vmem(part) for part in held], in_hbm(chol_vectors))
 
 
 def pieces_of(value, count):
@@ -161,12 +208,13 @@
     shape = (size, size)
     one = jnp.where(lax.broadcasted_iota(jnp.int32, shape, 0) == lax.broadcasted_iota(jnp.int32, shape, 1), 1.0, 0.0)
     largest = jnp.max(jnp.sum(jnp.abs(matrix), axis=1, keepdims=True), axis=0, keepdims=True)
-    guess = one * (1.5 / largest)
+    scale = 1.5 / largest
+    guess = scale * (2.0 * one - scale * matrix)
     halves = pieces_of(matrix, 2)
 
     def rough(carry):
         count, _, x = carry
-        for _ in range(3):
+        for _ in range(4):
             rest = one - fine_dot(halves, pieces_of(x, 2))
             x = x + fine_dot(pieces_of(x, 2), pieces_of(rest, 2))
         return count + 1, jnp.sum(rest * rest), x
@@ -177,7 +225,7 @@
         return count + 1, jnp.sum(rest * rest), x + full_dot(x, rest)
 
     _, _, guess = lax.while_loop(
-        lambda c: jnp.logical_and(c[0] < 14, c[1] > 1e-4), rough, (jnp.int32(0), jnp.float32(1), guess)
+        lambda c: jnp.logical_and(c[0] < 10, c[1] > 1e-4), rough, (jnp.int32(0), jnp.float32(1), guess)
     )
     _, _, guess = lax.while_loop(
         lambda c: jnp.logical_and(c[0] < 6, c[1] > 1e-6), exact, (jnp.int32(0), jnp.float32(1), guess)
@@ -336,7 +384,8 @@
     lanes = walkers.shape[2]
     spread = jnp.broadcast_to(field_draws.reshape(1, slab_vectors // lanes, lanes), (walk, slab_vectors // lanes, lanes))
     draws = lax.all_to_all(spread, "walk", split_axis=0, concat_axis=0, tiled=True)
-    partial = partial_operators(draws, chol_vectors, planes)
+    held = preload(chol_vectors, PRELOADED, lanes)
+    partial = partial_operators(draws, chol_vectors, held, planes)
     rows = lax.all_to_all(partial, BOTH, split_axis=0, concat_axis=0, tiled=True)
     other_rows = lax.ppermute(rows, "walk", swap)
 

time: 101 us -> 101 us (level)
  blocking collectives: 32.2 us -> 18.1 us
  starting transfers between devices: 15.1 us -> 22.1 us
  waiting for transfers between devices: 11.1 us -> 16 us
  Pallas kernels: 36.4 us -> 37.9 us
    all_to_all x1 -> x0, blocking collectives: 13.5 us -> none  [per_device(): lax.all_to_all(spread, 'walk', split_axis=0, concat_axis=0, tiled=True)]
    all_to_all x0 -> x1, starting transfers between devices: none -> 7.05 us  [per_device(): lax.all_to_all(spread, 'walk', split_axis=0, concat_axis=0, tiled=True)]
    all_to_all x0 -> x1, waiting for transfers between devices: none -> 4.87 us  [per_device(): lax.all_to_all(spread, 'walk', split_axis=0, concat_axis=0, tiled=True)]
    pallas_call x1 -> x2, Pallas kernels: 10.2 us -> 11.7 us  [the longest x1 9.94 us: partial_operators(): pl.pallas_call(functools.partial(operator_kernel, planes, loaded), in_spe...]
  transfers between devices with their start and end apart: 10 -> 11, of which waited for: 5 -> 6; matrix products, arithmetic and copies ran while one was open for 2% -> 3% of each run, Pallas kernels for 30% -> 31%
where the time goes in v4:
time: 101 us; the launch traced here: 100 us
  Pallas kernels  37.9 us (38%)
  starting transfers between devices  22.1 us (22%)
  blocking collectives  18.1 us (18%)
  waiting for transfers between devices  16 us (16%)
  between operations  2.55 us (3%)
  other arithmetic  2.26 us (2%)
  local copies, waits for them, and re-layouts  1.31 us (1%)
    pallas_call x4, Pallas kernels, energies(): pl.pallas_call(functools.partial(energy_kernel, group, sub), in_specs=[vm...  19.5 us
    all_to_all x1, blocking collectives, per_device(): lax.all_to_all(partial, BOTH, split_axis=0, concat_axis=0, tiled=True)  18.1 us
    pallas_call x1, Pallas kernels, partial_operators(): pl.pallas_call(functools.partial(operator_kernel, planes, loaded), in_spe...  9.94 us
    ppermute x6, starting transfers between devices, send(): return lax.ppermute(array, BOTH, pairs)  9.17 us
    all_to_all x1, starting transfers between devices, per_device(): lax.all_to_all(spread, 'walk', split_axis=0, concat_axis=0, tiled=True)  7.05 us
    pallas_call x1, Pallas kernels, solve(): pl.pallas_call(functools.partial(solve_kernel, planes), in_specs=[vmem] *...  6.66 us
    all_to_all x1, waiting for transfers between devices, per_device(): came = lax.all_to_all(sent, BOTH, split_axis=0, concat_axis=0, tiled=True)  6.41 us
    all_to_all x1, starting transfers between devices, per_device(): came = lax.all_to_all(sent, BOTH, split_axis=0, concat_axis=0, tiled=True)  4.9 us
  transfers between devices with their start and end apart: 11, of which 6 were waited for; matrix products, arithmetic and copies ran while one was open for 3% of the time, Pallas kernels for 31%

profile of v4, /device:TPU:0, one launch (start us, length us, event | category | flops | bytes accessed | tf_op | source)
XLA Modules:
  0.0 100.2 jit_solution(7897001514633407674)
XLA Ops:
  0.6 0.5 collective-permute-start.2
  1.1 0.7 reduce.1
  1.9 0.6 broadcast_in_dim.17
  2.5 7.0 %all-to-all-start = ((bf16[16,8,128]{2,1,0:T(8,128)(2,1)}), bf16[16,8,128]{2,1,0:T(8,128)(2,1)S(1)}, u32[]{:S(2)}, u32[]{:S(2)}) async-start(bf16[16,8,128]{2,1,0:T(8,128)(2,1)} %broadcast_in_dim.17), calls=%async_computation | async-start | bytes 65536 | tf_op jit(solution)/shard_map/all_to_all | solution.py:386
  9.5 1.8 %preload.1 = (bf16[128,32,256]{2,1,0:T(8,128)(2,1)S(1)}, bf16[64,32,128]{2,1,0:T(8,128)(2,1)S(1)}) custom-call(bf16[1024,32,512]{2,1,0:T(8,128)(2,1)} %refs_2_.1), custom_call_target="tpu_custom_call" | custom-call | bytes 5242880 | tf_op jit(solution)/shard_map/preload/pallas_call | solution.py:85
  11.3 4.9 %all-to-all-done.draws_ref = bf16[16,8,128]{2,1,0:T(8,128)(2,1)S(1)} async-done(((bf16[16,8,128]{2,1,0:T(8,128)(2,1)}), bf16[16,8,128]{2,1,0:T(8,128)(2,1)S(1)}, u32[]{:S(2)}, u32[]{:S(2)}) %all-to-all-start) | async-done | bytes 32800 | tf_op jit(solution)/shard_map/all_to_all | solution.py:386
  16.2 9.9 %operators.1 = bf16[32,16,384]{2,1,0:T(8,128)(2,1)S(1)} custom-call(bf16[16,8,128]{2,1,0:T(8,128)(2,1)S(1)} %all-to-all-done.draws_ref, bf16[128,32,256]{2,1,0:T(8,128)(2,1)S(1)} %get-tuple-element.16.refs_0_, bf16[64,32,128]{2,1,0:T(8,128)(2,1)S(1)} %get-tuple-element.17.refs_1_, bf16[1024,32,512]{2,1,0:T(8,128)(2,1)} %refs_2_.1), custom_call_target="tpu_custom_call" | custom-call | flops 5368709120 | bytes 20971520 | tf_op jit(solution)/shard_map/operators/pallas_call | solution.py:164
  26.1 18.1 %all_to_all.19.own_rows_ref = bf16[32,16,384]{2,1,0:T(8,128)(2,1)S(1)} all-to-all(bf16[32,16,384]{2,1,0:T(8,128)(2,1)S(1)} %operators.1), channel_id=1, replica_groups=mesh['chol'=2,'walk'=16] {'chol','walk'}, dimensions={0} | all-to-all | bytes 786432 | tf_op jit(solution)/shard_map/all_to_all | solution.py:389
  44.2 0.5 collective-permute-start.1
  44.7 0.1 stack.44
  44.8 1.3 %collective-permute-done.1 = bf16[1,512,128]{2,1,0:T(8,128)(2,1)S(1)} collective-permute-done((bf16[1,512,128]{2,1,0:T(8,128)(2,1)S(1)}, bf16[1,512,128]{2,1,0:T(8,128)(2,1)S(1)}, u32[]{:S(2)}, u32[]{:S(2)}) %collective-permute-start.1) | collective-permute-done | bytes 131104 | tf_op jit(solution)/shard_map/ppermute | solution.py:382
  46.1 0.0 collective-permute-done.other_rows_ref
  46.1 6.7 %solve.1 = (f32[512,128]{1,0:T(8,128)S(1)}, bf16[512,128]{1,0:T(8,128)(2,1)S(1)}, bf16[64,128,512]{2,1,0:T(8,128)(2,1)S(1)}, bf16[64,128,512]{2,1,0:T(8,128)(2,1)S(1)}) custom-call(bf16[32,16,384]{2,1,0:T(8,128)(2,1)S(1)} %all_to_all.19.own_rows_ref, bf16[32,16,384]{2,1,0:T(8,128)(2,1)S(1)} %collective-permute-done.other_rows_ref, ...), custom_call_target="tpu_custom_call" | custom-call | flops 6000000000 | bytes 16777216 | tf_op jit(solution)/shard_map/solve/pallas_call | solution.py:297
  52.8 1.0 collective-permute-start.4
  53.7 4.0 %collective-permute-start.5 = (bf16[512,128]{1,0:T(8,128)(2,1)S(1)}, bf16[512,128]{1,0:T(8,128)(2,1)S(1)}, u32[]{:S(2)}, u32[]{:S(2)}) collective-permute-start(bf16[512,128]{1,0:T(8,128)(2,1)S(1)} %get-tuple-element.19), channel_id=1, source_target_pairs={{0,12},{2,14},{4,8},{6,10},{9,5},{11,7},{13,1},{15,3},{16,28},{18,... | collective-permute-start | bytes 393224 | tf_op jit(solution)/shard_map/ppermute | solution.py:379
  57.8 3.1 %collective-permute-start.3 = (f32[512,128]{1,0:T(8,128)S(1)}, f32[512,128]{1,0:T(8,128)S(1)}, u32[]{:S(2)}, u32[]{:S(2)}) collective-permute-start(f32[512,128]{1,0:T(8,128)S(1)} %get-tuple-element.18), channel_id=1, source_target_pairs={{0,16},{2,18},{4,20},{6,22},{8,24},{10,26},{12,28},{14,30},{17,1},... | collective-permute-start | bytes 786440 | tf_op jit(solution)/shard_map/ppermute | solution.py:379
  61.0 0.2 collective-permute-start.6
  61.2 4.8 %energies.4 = f32[2,8,128]{2,1,0:T(8,128)S(1)} custom-call(bf16[64,128,512]{2,1,0:T(8,128)(2,1)S(1)} %get-tuple-element.20.own_ref, bf16[64,128,512]{2,1,0:T(8,128)(2,1)S(1)} %get-tuple-element.21.other_ref, bf16[2,512,128]{2,1,0:T(8,128)(2,1)S(1)} %pad_maximum_fusion.refs_0_), custom_call_target="tpu_custom_call" | custom-call | flops 4294967296 | bytes 16777216 | tf_op jit(solution)/shard_map/energies/pallas_call | solution.py:348
  66.0 1.4 %collective-permute-done.6.refs_0_ = bf16[2,512,128]{2,1,0:T(8,128)(2,1)S(1)} collective-permute-done((bf16[2,512,128]{2,1,0:T(8,128)(2,1)S(1)}, bf16[2,512,128]{2,1,0:T(8,128)(2,1)S(1)}, u32[]{:S(2)}, u32[]{:S(2)}) %collective-permute-start.6) | collective-permute-done | bytes 262176 | tf_op jit(solution)/shard_map/ppermute | solution.py:379
  67.4 0.4 collective-permute-start.7
  67.8 4.8 %energies.5 = f32[2,8,128]{2,1,0:T(8,128)S(1)} custom-call(bf16[64,128,512]{2,1,0:T(8,128)(2,1)S(1)} %get-tuple-element.20.own_ref, bf16[64,128,512]{2,1,0:T(8,128)(2,1)S(1)} %get-tuple-element.21.other_ref, bf16[2,512,128]{2,1,0:T(8,128)(2,1)S(1)} %collective-permute-done.6.refs_0_), custom_call_target="tpu_custom_call" | custom-call | flops 4294967296 | bytes 16777216 | tf_op jit(solution)/shard_map/energies/pallas_call | solution.py:348
  72.6 1.2 %collective-permute-done.7.refs_0_ = bf16[2,512,128]{2,1,0:T(8,128)(2,1)S(1)} collective-permute-done((bf16[2,512,128]{2,1,0:T(8,128)(2,1)S(1)}, bf16[2,512,128]{2,1,0:T(8,128)(2,1)S(1)}, u32[]{:S(2)}, u32[]{:S(2)}) %collective-permute-start.7) | collective-permute-done | bytes 262176 | tf_op jit(solution)/shard_map/ppermute | solution.py:379
  73.8 0.6 collective-permute-start.8
  74.4 5.1 %energies.6 = f32[2,8,128]{2,1,0:T(8,128)S(1)} custom-call(bf16[64,128,512]{2,1,0:T(8,128)(2,1)S(1)} %get-tuple-element.20.own_ref, bf16[64,128,512]{2,1,0:T(8,128)(2,1)S(1)} %get-tuple-element.21.other_ref, bf16[2,512,128]{2,1,0:T(8,128)(2,1)S(1)} %collective-permute-done.7.refs_0_), custom_call_target="tpu_custom_call" | custom-call | flops 4294967296 | bytes 16777216 | tf_op jit(solution)/shard_map/energies/pallas_call | solution.py:348
  79.4 0.8 collective-permute-done.8.refs_0_
  80.2 4.8 %energies.7 = f32[2,8,128]{2,1,0:T(8,128)S(1)} custom-call(bf16[64,128,512]{2,1,0:T(8,128)(2,1)S(1)} %get-tuple-element.20.own_ref, bf16[64,128,512]{2,1,0:T(8,128)(2,1)S(1)} %get-tuple-element.21.other_ref, bf16[2,512,128]{2,1,0:T(8,128)(2,1)S(1)} %collective-permute-done.8.refs_0_), custom_call_target="tpu_custom_call" | custom-call | flops 4294967296 | bytes 16777216 | tf_op jit(solution)/shard_map/energies/pallas_call | solution.py:348
  85.0 0.1 multiply_reduce_fusion
  85.1 0.6 broadcast_in_dim.19
  85.7 4.9 %all-to-all-start.2 = ((f32[32,1,128]{2,1,0:T(1,128)}), f32[32,1,128]{2,1,0:T(1,128)S(1)}, u32[]{:S(2)}, u32[]{:S(2)}) async-start(f32[32,1,128]{2,1,0:T(1,128)} %bitcast.13), calls=%async_computation.2 | async-start | bytes 32768 | tf_op jit(solution)/shard_map/all_to_all | solution.py:433
  90.6 0.7 select_bitcast_fusion
  91.4 6.4 %all-to-all-done.2 = f32[32,1,128]{2,1,0:T(1,128)S(1)} async-done(((f32[32,1,128]{2,1,0:T(1,128)}), f32[32,1,128]{2,1,0:T(1,128)S(1)}, u32[]{:S(2)}, u32[]{:S(2)}) %all-to-all-start.2) | async-done | bytes 16416 | tf_op jit(solution)/shard_map/all_to_all | solution.py:433
  97.8 0.6 reduce_sum.29
  (11 shorter events, 0.1 us)
Async XLA Ops:
  0.6 45.5 %collective-permute-start.2 = (bf16[64,128,512]{2,1,0:T(8,128)(2,1)}, bf16[64,128,512]{2,1,0:T(8,128)(2,1)}, u32[]{:S(2)}, u32[]{:S(2)}) collective-permute-start(bf16[64,128,512]{2,1,0:T(8,128)(2,1)} %own_ref.1), channel_id=1, source_target_pairs={{0,1},{1,0},{2,3},{3,2},{4,5},{5,4},{6,7},{7,6},{8,9},{9,8},{10,11... | collective-permute-start | bytes 25165832 | tf_op jit(solution)/shard_map/ppermute | solution.py:381
  2.5 13.7 %all-to-all-start = ((bf16[16,8,128]{2,1,0:T(8,128)(2,1)}), bf16[16,8,128]{2,1,0:T(8,128)(2,1)S(1)}, u32[]{:S(2)}, u32[]{:S(2)}) async-start(bf16[16,8,128]{2,1,0:T(8,128)(2,1)} %broadcast_in_dim.17), calls=%async_computation | async-start | bytes 65536 | tf_op jit(solution)/shard_map/all_to_all | solution.py:386
  16.2 28.0 %copy-start = (bf16[1,512,128]{2,1,0:T(8,128)(2,1)S(1)}, bf16[1,512,128]{2,1,0:T(8,128)(2,1)}, u32[]{:S(2)}) copy-start(bf16[1,512,128]{2,1,0:T(8,128)(2,1)} %param.7) | copy-start | bytes 393220
  44.2 1.9 %collective-permute-start = (bf16[32,16,384]{2,1,0:T(8,128)(2,1)S(1)}, bf16[32,16,384]{2,1,0:T(8,128)(2,1)S(1)}, u32[]{:S(2)}, u32[]{:S(2)}) collective-permute-start(bf16[32,16,384]{2,1,0:T(8,128)(2,1)S(1)} %all_to_all.19.own_rows_ref), channel_id=1, source_target_pairs={{0,1},{1,0},{2,3},{3,2},{4,5},{5,4},{6,7},{7,6},{8,9},{9,8},{10,11... | collective-permute-start | bytes 1179656 | tf_op jit(solution)/shard_map/ppermute | solution.py:390
  44.2 1.9 %collective-permute-start.1 = (bf16[1,512,128]{2,1,0:T(8,128)(2,1)S(1)}, bf16[1,512,128]{2,1,0:T(8,128)(2,1)S(1)}, u32[]{:S(2)}, u32[]{:S(2)}) collective-permute-start(bf16[1,512,128]{2,1,0:T(8,128)(2,1)S(1)} %copy-done), channel_id=1, source_target_pairs={{0,1},{1,0},{2,3},{3,2},{4,5},{5,4},{6,7},{7,6},{8,9},{9,8},{10,11... | collective-permute-start | bytes 393224 | tf_op jit(solution)/shard_map/ppermute | solution.py:382
  52.8 8.1 %collective-permute-start.4 = (bf16[512,128]{1,0:T(8,128)(2,1)S(1)}, bf16[512,128]{1,0:T(8,128)(2,1)S(1)}, u32[]{:S(2)}, u32[]{:S(2)}) collective-permute-start(bf16[512,128]{1,0:T(8,128)(2,1)S(1)} %get-tuple-element.19), channel_id=1, source_target_pairs={{0,4},{1,8},{2,6},{3,10},{4,0},{5,12},{6,2},{7,14},{8,1},{9,13},{1... | collective-permute-start | bytes 393224 | tf_op jit(solution)/shard_map/ppermute | solution.py:379
  53.7 7.2 %collective-permute-start.5 = (bf16[512,128]{1,0:T(8,128)(2,1)S(1)}, bf16[512,128]{1,0:T(8,128)(2,1)S(1)}, u32[]{:S(2)}, u32[]{:S(2)}) collective-permute-start(bf16[512,128]{1,0:T(8,128)(2,1)S(1)} %get-tuple-element.19), channel_id=1, source_target_pairs={{0,12},{2,14},{4,8},{6,10},{9,5},{11,7},{13,1},{15,3},{16,28},{18,... | collective-permute-start | bytes 393224 | tf_op jit(solution)/shard_map/ppermute | solution.py:379
  57.8 32.9 %collective-permute-start.3 = (f32[512,128]{1,0:T(8,128)S(1)}, f32[512,128]{1,0:T(8,128)S(1)}, u32[]{:S(2)}, u32[]{:S(2)}) collective-permute-start(f32[512,128]{1,0:T(8,128)S(1)} %get-tuple-element.18), channel_id=1, source_target_pairs={{0,16},{2,18},{4,20},{6,22},{8,24},{10,26},{12,28},{14,30},{17,1},... | collective-permute-start | bytes 786440 | tf_op jit(solution)/shard_map/ppermute | solution.py:379
  61.0 6.4 %collective-permute-start.6 = (bf16[2,512,128]{2,1,0:T(8,128)(2,1)S(1)}, bf16[2,512,128]{2,1,0:T(8,128)(2,1)S(1)}, u32[]{:S(2)}, u32[]{:S(2)}) collective-permute-start(bf16[2,512,128]{2,1,0:T(8,128)(2,1)S(1)} %pad_maximum_fusion.refs_0_), channel_id=1, source_target_pairs={{0,2},{1,17},{2,0},{3,19},{4,6},{5,21},{6,4},{7,23},{8,10},{9,25},... | collective-permute-start | bytes 786440 | tf_op jit(solution)/shard_map/ppermute | solution.py:379
  67.4 6.4 %collective-permute-start.7 = (bf16[2,512,128]{2,1,0:T(8,128)(2,1)S(1)}, bf16[2,512,128]{2,1,0:T(8,128)(2,1)S(1)}, u32[]{:S(2)}, u32[]{:S(2)}) collective-permute-start(bf16[2,512,128]{2,1,0:T(8,128)(2,1)S(1)} %pad_maximum_fusion.refs_0_), channel_id=1, source_target_pairs={{0,16},{1,3},{2,18},{3,1},{4,20},{5,7},{6,22},{7,5},{8,24},{9,11},... | collective-permute-start | bytes 786440 | tf_op jit(solution)/shard_map/ppermute | solution.py:379
  73.8 6.4 %collective-permute-start.8 = (bf16[2,512,128]{2,1,0:T(8,128)(2,1)S(1)}, bf16[2,512,128]{2,1,0:T(8,128)(2,1)S(1)}, u32[]{:S(2)}, u32[]{:S(2)}) collective-permute-start(bf16[2,512,128]{2,1,0:T(8,128)(2,1)S(1)} %collective-permute-done.6.refs_0_), channel_id=1, source_target_pairs={{0,16},{1,3},{2,18},{3,1},{4,20},{5,7},{6,22},{7,5},{8,24},{9,11},... | collective-permute-start | bytes 786440 | tf_op jit(solution)/shard_map/ppermute | solution.py:379
  85.7 12.1 %all-to-all-start.2 = ((f32[32,1,128]{2,1,0:T(1,128)}), f32[32,1,128]{2,1,0:T(1,128)S(1)}, u32[]{:S(2)}, u32[]{:S(2)}) async-start(f32[32,1,128]{2,1,0:T(1,128)} %bitcast.13), calls=%async_computation.2 | async-start | bytes 32768 | tf_op jit(solution)/shard_map/all_to_all | solution.py:433
